TPU v7x, 256 devices: a whole 4x4x8 slice. The times are simulated.
256 devices in a mesh: ctx: 16 (over y_lo, z), seq: 16 (over y_hi, x, core).
Axes of the slice: x: 4, y: 4 (y_hi: 2, y_lo: 2; y = y_hi * 2 + y_lo), z: 8, core: 2. Of those that a mesh axis runs over, the one named last changes fastest.
Arguments:
- queries: bfloat16 [65536, 1024], P(('seq', 'ctx')), parts along dimension 0, may hold values from -40 to 40
- keys: bfloat16 [65536, 128], P(('seq', 'ctx')), parts along dimension 0, may hold values from -40 to 40
- values: bfloat16 [65536, 128], P(('seq', 'ctx')), parts along dimension 0, may hold values from -6 to 6
- attn_out: bfloat16 [65536, 1024], P(('seq', 'ctx')), parts along dimension 0, may hold values from -4 to 4
- out_grad: bfloat16 [65536, 1024], P(('seq', 'ctx')), parts along dimension 0, may hold values from -6 to 6
- tile_doc: int32 [512], P('seq'), parts along dimension 0, may hold values from 0 to 7, never falling along the last dimension, each value on 1 to 24 neighbouring positions
Outputs:
- query_grad: bfloat16 [65536, 1024], P(('seq', 'ctx')), parts along dimension 0
- key_grad: bfloat16 [65536, 128], P(('seq', 'ctx')), parts along dimension 0
- value_grad: bfloat16 [65536, 128], P(('seq', 'ctx')), parts along dimension 0
There are 16 independent parts, one for each index of `seq`. A program takes and returns all parts, laid end to end along the dimension named above; each array names one. Nothing has to cross between parts.
Inputs may be any that keep to these rules, and one draw needn't show every extreme that they name: tile_doc never falls; every document covers 1 to 24 consecutive tiles and one covers exactly 24.
All inputs are finite; a program needn't handle non-finite values.
Results may differ from a plain program's by a relative error of at most 0.005.
Values may be sent and summed in bfloat16 or wider, within the bound.
A program may use at most 128 MiB of HBM per device.

v0:
```python
import math

import jax
import jax.numpy as jnp
from jax import lax
from jax.sharding import PartitionSpec as P

HEADS = 8
TILE = 128


masked_fill = -1e30


def passed_along(shard, axis, by):
    length = lax.axis_size(axis)
    pairs = [(i, i + by) for i in range(length) if 0 <= i + by < length]
    return lax.ppermute(shard, axis, pairs)


def local(queries, keys, values, attn_out, out_grad, tile_doc):
    row_count = queries.shape[0]
    head_width = keys.shape[1]
    ctx_count = lax.axis_size("ctx")
    my_index = lax.axis_index("ctx")
    seq_rows = row_count * ctx_count
    score_scale = 1.0 / math.sqrt(head_width)
    token_doc = jnp.repeat(tile_doc, TILE)
    query_first = my_index * row_count
    query_pos = query_first + jnp.arange(row_count, dtype=jnp.int32)
    query_doc = lax.dynamic_slice_in_dim(token_doc, query_first, row_count, 0)
    query_three = queries.reshape(row_count, HEADS, head_width)
    grad_three = out_grad.reshape(row_count, HEADS, head_width)
    delta = jnp.transpose(
        jnp.sum(
            (out_grad.astype(jnp.float32) * attn_out.astype(jnp.float32)).reshape(
                row_count, HEADS, head_width
            ),
            axis=-1,
        )
    )[:, :, None]

    def allowed_for(key_first, key_count):
        key_pos = key_first + jnp.arange(key_count, dtype=jnp.int32)
        key_doc = lax.dynamic_slice_in_dim(
            token_doc, jnp.clip(key_first, 0, seq_rows - key_count), key_count, 0
        )
        inside = key_first >= 0
        return (
            (query_doc[:, None] == key_doc[None, :])
            & (key_pos[None, :] <= query_pos[:, None])
            & inside
        )

    def grad_step(key_rows, value_rows, key_first, log_norm):
        key_count = key_rows.shape[0]
        allowed = allowed_for(key_first, key_count)
        scores = (
            jnp.einsum("qhe,ke->hqk", query_three, key_rows, preferred_element_type=jnp.float32)
            * score_scale
        )
        weights = jnp.where(allowed[None], jnp.exp(scores - log_norm), 0.0)
        weights_round = weights.astype(jnp.bfloat16)
        dprob = jnp.einsum(
            "qhe,ke->hqk", grad_three, value_rows, preferred_element_type=jnp.float32
        )
        dscore_round = (weights * (dprob - delta)).astype(jnp.bfloat16)
        query_part = jnp.einsum(
            "hqk,ke->qhe", dscore_round, key_rows, preferred_element_type=jnp.float32
        )
        key_part = jnp.einsum(
            "hqk,qhe->ke", dscore_round, query_three, preferred_element_type=jnp.float32
        )
        value_part = jnp.einsum(
            "hqk,qhe->ke", weights_round, grad_three, preferred_element_type=jnp.float32
        )
        return (query_part, key_part, value_part)

    key_rows = lax.all_gather(keys, "ctx", axis=0, tiled=True)
    row_max = jnp.full((HEADS, row_count, 1), masked_fill, jnp.float32)
    allowed = allowed_for(jnp.int32(0), key_rows.shape[0])
    scores = (
        jnp.einsum("qhe,ke->hqk", query_three, key_rows, preferred_element_type=jnp.float32)
        * score_scale
    )
    masked = jnp.where(allowed[None], scores, masked_fill)
    new_max = jnp.maximum(row_max, jnp.max(masked, axis=-1, keepdims=True))
    added = jnp.sum(
        jnp.where(allowed[None], jnp.exp(masked - new_max), 0.0), axis=-1, keepdims=True
    )
    log_norm = new_max + jnp.log(added)
    query_part, key_part, value_part = grad_step(keys, values, query_first, log_norm)
    key_store = jnp.zeros((ctx_count, row_count, head_width), jnp.float32).at[0].set(key_part)
    value_store = jnp.zeros((ctx_count, row_count, head_width), jnp.float32).at[0].set(value_part)

    def forward_turn(turn_index, state):
        key_rows, value_rows, key_store, value_store, query_acc = state
        key_rows, value_rows = passed_along((key_rows, value_rows), "ctx", 1)
        owner_first = (my_index - turn_index) * row_count
        query_part, key_part, value_part = grad_step(key_rows, value_rows, owner_first, log_norm)
        key_store = lax.dynamic_update_index_in_dim(key_store, key_part, turn_index, 0)
        value_store = lax.dynamic_update_index_in_dim(value_store, value_part, turn_index, 0)
        return (key_rows, value_rows, key_store, value_store, query_acc + query_part)

    state = lax.fori_loop(
        1, ctx_count, forward_turn, (keys, values, key_store, value_store, query_part)
    )
    key_store, value_store, query_acc = (state[2], state[3], state[4])

    def return_turn(step_index, sums):
        section = ctx_count - 2 - step_index
        key_sum, value_sum = passed_along((sums[0], sums[1]), "ctx", -1)
        key_sum = key_sum + lax.dynamic_index_in_dim(key_store, section, 0, keepdims=False)
        value_sum = value_sum + lax.dynamic_index_in_dim(value_store, section, 0, keepdims=False)
        return (key_sum, value_sum)

    last_sums = (key_store[ctx_count - 1], value_store[ctx_count - 1])
    key_sum, value_sum = lax.fori_loop(0, ctx_count - 1, return_turn, last_sums)
    query_grad = (
        (query_acc * score_scale).reshape(row_count, HEADS * head_width).astype(jnp.bfloat16)
    )
    key_grad = (key_sum * score_scale).astype(jnp.bfloat16)
    value_grad = value_sum.astype(jnp.bfloat16)
    return (query_grad, key_grad, value_grad)


def solution(mesh):
    in_specs = (
        P(("seq", "ctx"), None),
        P(("seq", "ctx"), None),
        P(("seq", "ctx"), None),
        P(("seq", "ctx"), None),
        P(("seq", "ctx"), None),
        P("seq"),
    )
    out_specs = (P(("seq", "ctx"), None), P(("seq", "ctx"), None), P(("seq", "ctx"), None))
    return jax.shard_map(local, mesh=mesh, in_specs=in_specs, out_specs=out_specs, check_vma=False)
```

profile of v0, /device:TPU:8, one launch (start us, length us, event | category | flops | bytes accessed | tf_op | source)
XLA Modules:
  0.0 499.8 jit_solution(4576737142179178578)
XLA Ops:
  15.8 65.8 %all-gather.2.cloned.1.call-done = bf16[4096,128]{1,0:T(8,128)(2,1)} async-done(((bf16[256,128]{1,0:T(8,128)(2,1)}), bf16[4096,128]{1,0:T(8,128)(2,1)}) %all-gather.2.cloned.1.call-update) | async-done | bytes 1048592 | tf_op jit(solution)/shard_map/all_gather | solution.py:79
  81.6 14.7 %fusion.13 = (f32[8,256]{1,0:T(8,128)S(1)}, f32[4096,256,8]{1,0,2:T(8,128)}) fusion(pred[256,4096]{0,1:T(8,128)(4,1)S(1)} %fusion.14, bf16[256,8,128]{0,2,1:T(8,128)(2,1)S(1)} %bitcast.149, bf16[4096,128]{1,0:T(8,128)(2,1)} %all-gather.2.cloned.1.call-done), kind=kOutput, calls=%fused_computation.24 | convolution fusion | flops 2172647424 | bytes 36184064 | tf_op jit(solution)/shard_map/qhe,ke->hqk/dot_general | solution.py:83
  96.3 14.9 %select_reduce_fusion = f32[8,256]{1,0:T(8,128)S(1)} fusion(f32[4096,256,8]{1,0,2:T(8,128)} %get-tuple-element.597, f32[8,256]{1,0:T(8,128)S(1)} %broadcast_maximum_fusion, pred[256,4096]{0,1:T(8,128)(4,1)S(1)} %fusion.14), kind=kLoop, calls=%fused_computation.23 | loop fusion | flops 41940992 | bytes 34619392 | tf_op jit(solution)/shard_map/reduce_sum | solution.py:88
  116.7 188.3 %while.44 = (s32[]{:T(128)}, bf16[256,128]{1,0:T(8,128)(2,1)S(1)}, bf16[256,128]{1,0:T(8,128)(2,1)S(1)}, f32[16,256,128]{2,1,0:T(8,128)}, f32[16,256,128]{2,1,0:...) while((s32[]{:T(128)}, bf16[256,128]{1,0:T(8,128)(2,1)S(1)}, ...), condition=%wide.region_4.5_spmd.clone, body=%wide.region_3.4_spmd.clone.sunk | while | flops 675283456 | bytes 15032693 | solution.py:105
  116.7 2.6 collective-permute-start.2
  121.5 3.8 collective-permute-done.2
  134.3 4.1 collective-permute-done.2
  146.7 4.4 collective-permute-done.2
  159.2 4.1 collective-permute-done.2
  171.6 4.1 collective-permute-done.2
  184.0 4.1 collective-permute-done.2
  196.4 4.1 collective-permute-done.2
  208.8 4.1 collective-permute-done.2
  221.2 4.1 collective-permute-done.2
  233.6 4.1 collective-permute-done.2
  246.3 4.4 collective-permute-done.2
  259.0 4.1 collective-permute-done.2
  271.5 4.8 collective-permute-done.2
  284.3 4.1 collective-permute-done.2
  296.7 4.1 collective-permute-done.2
  305.9 184.9 %while.43 = (s32[]{:T(128)}, f32[256,128]{1,0:T(8,128)S(1)}, f32[256,128]{1,0:T(8,128)S(1)}, f32[16,256,128]{2,1,0:T(8,128)}, f32[16,256,128]{2,1,0:T(8,128)}, /*index=5*/s32[]{:T(128)}, s32[]{:T(128)}, s32[]{:T(128)}, s32[]{:T(128)}) while((s32[]{:T(128)}, f32[256,128]{1,0:T(8,128)S(1)}, f32[256,128]{1,0:T(8,128)S(1)}, ...), condition=%wide.region_6.7_spmd, body=%wide.region_5.6_spmd.sunk | while | flops 65542 | bytes 1835235 | solution.py:118
  306.0 3.9 collective-permute-start.1
  313.8 3.9 collective-permute-done
  318.6 3.1 collective-permute-start.1
  329.5 4.7 collective-permute-start.1
  338.1 3.8 collective-permute-done
  342.8 4.7 collective-permute-start.1
  352.3 2.9 collective-permute-done
  356.2 5.2 %collective-permute-start.1 = (f32[256,128]{1,0:T(8,128)S(1)}, f32[256,128]{1,0:T(8,128)S(1)}, u32[]{:S(2)}, u32[]{:S(2)}) collective-permute-start(f32[256,128]{1,0:T(8,128)S(1)} %get-tuple-element.784), channel_id=1, source_target_pairs={{16,0},{32,16},{48,32},{64,48},{80,64},{96,80},{112,96},{128,112},... | collective-permute-start | bytes 393224 | tf_op jit(solution)/shard_map/while/body/eval_jaxpr/ppermute | solution.py:18
  365.9 2.3 collective-permute-done
  369.2 5.2 %collective-permute-start.1 = (f32[256,128]{1,0:T(8,128)S(1)}, f32[256,128]{1,0:T(8,128)S(1)}, u32[]{:S(2)}, u32[]{:S(2)}) collective-permute-start(f32[256,128]{1,0:T(8,128)S(1)} %get-tuple-element.784), channel_id=1, source_target_pairs={{16,0},{32,16},{48,32},{64,48},{80,64},{96,80},{112,96},{128,112},... | collective-permute-start | bytes 393224 | tf_op jit(solution)/shard_map/while/body/eval_jaxpr/ppermute | solution.py:18
  382.2 4.9 collective-permute-start.1
  391.7 2.2 collective-permute-done
  394.9 4.7 collective-permute-start.1
  403.9 2.6 collective-permute-done
  407.4 4.4 collective-permute-start.1
  415.9 2.8 collective-permute-done
  419.7 4.1 collective-permute-start.1
  428.0 2.7 collective-permute-done
  431.6 4.0 collective-permute-start.1
  443.4 4.0 collective-permute-start.1
  451.7 2.6 collective-permute-done
  455.3 4.0 collective-permute-start.1
  463.1 3.1 collective-permute-done
  467.1 4.0 collective-permute-start.1
  474.9 3.1 collective-permute-done
  479.0 4.0 collective-permute-start.1
  486.8 3.1 collective-permute-done
  (311 shorter events, 222.2 us)
Async XLA Ops:
  7.2 74.4 %all-gather.2.cloned.1.call-start = ((), (), s32[]{:S(2)}) async-start(), calls=%async_computation | async-start | bytes 1114112 | tf_op jit(solution)/shard_map/all_gather | solution.py:79
  116.7 8.7 %collective-permute-start.2 = (bf16[256,128]{1,0:T(8,128)(2,1)S(1)}, bf16[256,128]{1,0:T(8,128)(2,1)S(1)}, u32[]{:S(2)}, u32[]{:S(2)}) collective-permute-start(bf16[256,128]{1,0:T(8,128)(2,1)S(1)} %get-tuple-element.736), channel_id=1, source_target_pairs={{0,16},{16,32},{32,48},{48,64},{64,80},{80,96},{96,112},{112,128},... | collective-permute-start | bytes 196616 | tf_op jit(solution)/shard_map/while/body/eval_jaxpr/ppermute | solution.py:18
  119.3 8.6 %collective-permute-start.3 = (bf16[256,128]{1,0:T(8,128)(2,1)S(1)}, bf16[256,128]{1,0:T(8,128)(2,1)S(1)}, u32[]{:S(2)}, u32[]{:S(2)}) collective-permute-start(bf16[256,128]{1,0:T(8,128)(2,1)S(1)} %get-tuple-element.737), channel_id=1, source_target_pairs={{0,16},{16,32},{32,48},{48,64},{64,80},{80,96},{96,112},{112,128},... | collective-permute-start | bytes 196616 | tf_op jit(solution)/shard_map/while/body/eval_jaxpr/ppermute | solution.py:18
  130.2 8.3 %collective-permute-start.2 = (bf16[256,128]{1,0:T(8,128)(2,1)S(1)}, bf16[256,128]{1,0:T(8,128)(2,1)S(1)}, u32[]{:S(2)}, u32[]{:S(2)}) collective-permute-start(bf16[256,128]{1,0:T(8,128)(2,1)S(1)} %get-tuple-element.736), channel_id=1, source_target_pairs={{0,16},{16,32},{32,48},{48,64},{64,80},{80,96},{96,112},{112,128},... | collective-permute-start | bytes 196616 | tf_op jit(solution)/shard_map/while/body/eval_jaxpr/ppermute | solution.py:18
  132.1 8.3 %collective-permute-start.3 = (bf16[256,128]{1,0:T(8,128)(2,1)S(1)}, bf16[256,128]{1,0:T(8,128)(2,1)S(1)}, u32[]{:S(2)}, u32[]{:S(2)}) collective-permute-start(bf16[256,128]{1,0:T(8,128)(2,1)S(1)} %get-tuple-element.737), channel_id=1, source_target_pairs={{0,16},{16,32},{32,48},{48,64},{64,80},{80,96},{96,112},{112,128},... | collective-permute-start | bytes 196616 | tf_op jit(solution)/shard_map/while/body/eval_jaxpr/ppermute | solution.py:18
  142.6 8.5 %collective-permute-start.2 = (bf16[256,128]{1,0:T(8,128)(2,1)S(1)}, bf16[256,128]{1,0:T(8,128)(2,1)S(1)}, u32[]{:S(2)}, u32[]{:S(2)}) collective-permute-start(bf16[256,128]{1,0:T(8,128)(2,1)S(1)} %get-tuple-element.736), channel_id=1, source_target_pairs={{0,16},{16,32},{32,48},{48,64},{64,80},{80,96},{96,112},{112,128},... | collective-permute-start | bytes 196616 | tf_op jit(solution)/shard_map/while/body/eval_jaxpr/ppermute | solution.py:18
  144.5 8.3 %collective-permute-start.3 = (bf16[256,128]{1,0:T(8,128)(2,1)S(1)}, bf16[256,128]{1,0:T(8,128)(2,1)S(1)}, u32[]{:S(2)}, u32[]{:S(2)}) collective-permute-start(bf16[256,128]{1,0:T(8,128)(2,1)S(1)} %get-tuple-element.737), channel_id=1, source_target_pairs={{0,16},{16,32},{32,48},{48,64},{64,80},{80,96},{96,112},{112,128},... | collective-permute-start | bytes 196616 | tf_op jit(solution)/shard_map/while/body/eval_jaxpr/ppermute | solution.py:18
  155.0 8.3 %collective-permute-start.2 = (bf16[256,128]{1,0:T(8,128)(2,1)S(1)}, bf16[256,128]{1,0:T(8,128)(2,1)S(1)}, u32[]{:S(2)}, u32[]{:S(2)}) collective-permute-start(bf16[256,128]{1,0:T(8,128)(2,1)S(1)} %get-tuple-element.736), channel_id=1, source_target_pairs={{0,16},{16,32},{32,48},{48,64},{64,80},{80,96},{96,112},{112,128},... | collective-permute-start | bytes 196616 | tf_op jit(solution)/shard_map/while/body/eval_jaxpr/ppermute | solution.py:18
  156.9 8.3 %collective-permute-start.3 = (bf16[256,128]{1,0:T(8,128)(2,1)S(1)}, bf16[256,128]{1,0:T(8,128)(2,1)S(1)}, u32[]{:S(2)}, u32[]{:S(2)}) collective-permute-start(bf16[256,128]{1,0:T(8,128)(2,1)S(1)} %get-tuple-element.737), channel_id=1, source_target_pairs={{0,16},{16,32},{32,48},{48,64},{64,80},{80,96},{96,112},{112,128},... | collective-permute-start | bytes 196616 | tf_op jit(solution)/shard_map/while/body/eval_jaxpr/ppermute | solution.py:18
  167.4 8.3 %collective-permute-start.2 = (bf16[256,128]{1,0:T(8,128)(2,1)S(1)}, bf16[256,128]{1,0:T(8,128)(2,1)S(1)}, u32[]{:S(2)}, u32[]{:S(2)}) collective-permute-start(bf16[256,128]{1,0:T(8,128)(2,1)S(1)} %get-tuple-element.736), channel_id=1, source_target_pairs={{0,16},{16,32},{32,48},{48,64},{64,80},{80,96},{96,112},{112,128},... | collective-permute-start | bytes 196616 | tf_op jit(solution)/shard_map/while/body/eval_jaxpr/ppermute | solution.py:18
  169.3 8.3 %collective-permute-start.3 = (bf16[256,128]{1,0:T(8,128)(2,1)S(1)}, bf16[256,128]{1,0:T(8,128)(2,1)S(1)}, u32[]{:S(2)}, u32[]{:S(2)}) collective-permute-start(bf16[256,128]{1,0:T(8,128)(2,1)S(1)} %get-tuple-element.737), channel_id=1, source_target_pairs={{0,16},{16,32},{32,48},{48,64},{64,80},{80,96},{96,112},{112,128},... | collective-permute-start | bytes 196616 | tf_op jit(solution)/shard_map/while/body/eval_jaxpr/ppermute | solution.py:18
  179.8 8.3 %collective-permute-start.2 = (bf16[256,128]{1,0:T(8,128)(2,1)S(1)}, bf16[256,128]{1,0:T(8,128)(2,1)S(1)}, u32[]{:S(2)}, u32[]{:S(2)}) collective-permute-start(bf16[256,128]{1,0:T(8,128)(2,1)S(1)} %get-tuple-element.736), channel_id=1, source_target_pairs={{0,16},{16,32},{32,48},{48,64},{64,80},{80,96},{96,112},{112,128},... | collective-permute-start | bytes 196616 | tf_op jit(solution)/shard_map/while/body/eval_jaxpr/ppermute | solution.py:18
  181.8 8.3 %collective-permute-start.3 = (bf16[256,128]{1,0:T(8,128)(2,1)S(1)}, bf16[256,128]{1,0:T(8,128)(2,1)S(1)}, u32[]{:S(2)}, u32[]{:S(2)}) collective-permute-start(bf16[256,128]{1,0:T(8,128)(2,1)S(1)} %get-tuple-element.737), channel_id=1, source_target_pairs={{0,16},{16,32},{32,48},{48,64},{64,80},{80,96},{96,112},{112,128},... | collective-permute-start | bytes 196616 | tf_op jit(solution)/shard_map/while/body/eval_jaxpr/ppermute | solution.py:18
  192.3 8.3 %collective-permute-start.2 = (bf16[256,128]{1,0:T(8,128)(2,1)S(1)}, bf16[256,128]{1,0:T(8,128)(2,1)S(1)}, u32[]{:S(2)}, u32[]{:S(2)}) collective-permute-start(bf16[256,128]{1,0:T(8,128)(2,1)S(1)} %get-tuple-element.736), channel_id=1, source_target_pairs={{0,16},{16,32},{32,48},{48,64},{64,80},{80,96},{96,112},{112,128},... | collective-permute-start | bytes 196616 | tf_op jit(solution)/shard_map/while/body/eval_jaxpr/ppermute | solution.py:18
  194.2 8.3 %collective-permute-start.3 = (bf16[256,128]{1,0:T(8,128)(2,1)S(1)}, bf16[256,128]{1,0:T(8,128)(2,1)S(1)}, u32[]{:S(2)}, u32[]{:S(2)}) collective-permute-start(bf16[256,128]{1,0:T(8,128)(2,1)S(1)} %get-tuple-element.737), channel_id=1, source_target_pairs={{0,16},{16,32},{32,48},{48,64},{64,80},{80,96},{96,112},{112,128},... | collective-permute-start | bytes 196616 | tf_op jit(solution)/shard_map/while/body/eval_jaxpr/ppermute | solution.py:18
  204.7 8.3 %collective-permute-start.2 = (bf16[256,128]{1,0:T(8,128)(2,1)S(1)}, bf16[256,128]{1,0:T(8,128)(2,1)S(1)}, u32[]{:S(2)}, u32[]{:S(2)}) collective-permute-start(bf16[256,128]{1,0:T(8,128)(2,1)S(1)} %get-tuple-element.736), channel_id=1, source_target_pairs={{0,16},{16,32},{32,48},{48,64},{64,80},{80,96},{96,112},{112,128},... | collective-permute-start | bytes 196616 | tf_op jit(solution)/shard_map/while/body/eval_jaxpr/ppermute | solution.py:18
  206.6 8.3 %collective-permute-start.3 = (bf16[256,128]{1,0:T(8,128)(2,1)S(1)}, bf16[256,128]{1,0:T(8,128)(2,1)S(1)}, u32[]{:S(2)}, u32[]{:S(2)}) collective-permute-start(bf16[256,128]{1,0:T(8,128)(2,1)S(1)} %get-tuple-element.737), channel_id=1, source_target_pairs={{0,16},{16,32},{32,48},{48,64},{64,80},{80,96},{96,112},{112,128},... | collective-permute-start | bytes 196616 | tf_op jit(solution)/shard_map/while/body/eval_jaxpr/ppermute | solution.py:18
  217.1 8.3 %collective-permute-start.2 = (bf16[256,128]{1,0:T(8,128)(2,1)S(1)}, bf16[256,128]{1,0:T(8,128)(2,1)S(1)}, u32[]{:S(2)}, u32[]{:S(2)}) collective-permute-start(bf16[256,128]{1,0:T(8,128)(2,1)S(1)} %get-tuple-element.736), channel_id=1, source_target_pairs={{0,16},{16,32},{32,48},{48,64},{64,80},{80,96},{96,112},{112,128},... | collective-permute-start | bytes 196616 | tf_op jit(solution)/shard_map/while/body/eval_jaxpr/ppermute | solution.py:18
  219.0 8.3 %collective-permute-start.3 = (bf16[256,128]{1,0:T(8,128)(2,1)S(1)}, bf16[256,128]{1,0:T(8,128)(2,1)S(1)}, u32[]{:S(2)}, u32[]{:S(2)}) collective-permute-start(bf16[256,128]{1,0:T(8,128)(2,1)S(1)} %get-tuple-element.737), channel_id=1, source_target_pairs={{0,16},{16,32},{32,48},{48,64},{64,80},{80,96},{96,112},{112,128},... | collective-permute-start | bytes 196616 | tf_op jit(solution)/shard_map/while/body/eval_jaxpr/ppermute | solution.py:18
  229.5 8.3 %collective-permute-start.2 = (bf16[256,128]{1,0:T(8,128)(2,1)S(1)}, bf16[256,128]{1,0:T(8,128)(2,1)S(1)}, u32[]{:S(2)}, u32[]{:S(2)}) collective-permute-start(bf16[256,128]{1,0:T(8,128)(2,1)S(1)} %get-tuple-element.736), channel_id=1, source_target_pairs={{0,16},{16,32},{32,48},{48,64},{64,80},{80,96},{96,112},{112,128},... | collective-permute-start | bytes 196616 | tf_op jit(solution)/shard_map/while/body/eval_jaxpr/ppermute | solution.py:18
  231.4 8.5 %collective-permute-start.3 = (bf16[256,128]{1,0:T(8,128)(2,1)S(1)}, bf16[256,128]{1,0:T(8,128)(2,1)S(1)}, u32[]{:S(2)}, u32[]{:S(2)}) collective-permute-start(bf16[256,128]{1,0:T(8,128)(2,1)S(1)} %get-tuple-element.737), channel_id=1, source_target_pairs={{0,16},{16,32},{32,48},{48,64},{64,80},{80,96},{96,112},{112,128},... | collective-permute-start | bytes 196616 | tf_op jit(solution)/shard_map/while/body/eval_jaxpr/ppermute | solution.py:18
  242.2 8.6 %collective-permute-start.2 = (bf16[256,128]{1,0:T(8,128)(2,1)S(1)}, bf16[256,128]{1,0:T(8,128)(2,1)S(1)}, u32[]{:S(2)}, u32[]{:S(2)}) collective-permute-start(bf16[256,128]{1,0:T(8,128)(2,1)S(1)} %get-tuple-element.736), channel_id=1, source_target_pairs={{0,16},{16,32},{32,48},{48,64},{64,80},{80,96},{96,112},{112,128},... | collective-permute-start | bytes 196616 | tf_op jit(solution)/shard_map/while/body/eval_jaxpr/ppermute | solution.py:18
  244.1 8.6 %collective-permute-start.3 = (bf16[256,128]{1,0:T(8,128)(2,1)S(1)}, bf16[256,128]{1,0:T(8,128)(2,1)S(1)}, u32[]{:S(2)}, u32[]{:S(2)}) collective-permute-start(bf16[256,128]{1,0:T(8,128)(2,1)S(1)} %get-tuple-element.737), channel_id=1, source_target_pairs={{0,16},{16,32},{32,48},{48,64},{64,80},{80,96},{96,112},{112,128},... | collective-permute-start | bytes 196616 | tf_op jit(solution)/shard_map/while/body/eval_jaxpr/ppermute | solution.py:18
  254.9 8.3 %collective-permute-start.2 = (bf16[256,128]{1,0:T(8,128)(2,1)S(1)}, bf16[256,128]{1,0:T(8,128)(2,1)S(1)}, u32[]{:S(2)}, u32[]{:S(2)}) collective-permute-start(bf16[256,128]{1,0:T(8,128)(2,1)S(1)} %get-tuple-element.736), channel_id=1, source_target_pairs={{0,16},{16,32},{32,48},{48,64},{64,80},{80,96},{96,112},{112,128},... | collective-permute-start | bytes 196616 | tf_op jit(solution)/shard_map/while/body/eval_jaxpr/ppermute | solution.py:18
  256.8 8.3 %collective-permute-start.3 = (bf16[256,128]{1,0:T(8,128)(2,1)S(1)}, bf16[256,128]{1,0:T(8,128)(2,1)S(1)}, u32[]{:S(2)}, u32[]{:S(2)}) collective-permute-start(bf16[256,128]{1,0:T(8,128)(2,1)S(1)} %get-tuple-element.737), channel_id=1, source_target_pairs={{0,16},{16,32},{32,48},{48,64},{64,80},{80,96},{96,112},{112,128},... | collective-permute-start | bytes 196616 | tf_op jit(solution)/shard_map/while/body/eval_jaxpr/ppermute | solution.py:18
  267.3 8.9 %collective-permute-start.2 = (bf16[256,128]{1,0:T(8,128)(2,1)S(1)}, bf16[256,128]{1,0:T(8,128)(2,1)S(1)}, u32[]{:S(2)}, u32[]{:S(2)}) collective-permute-start(bf16[256,128]{1,0:T(8,128)(2,1)S(1)} %get-tuple-element.736), channel_id=1, source_target_pairs={{0,16},{16,32},{32,48},{48,64},{64,80},{80,96},{96,112},{112,128},... | collective-permute-start | bytes 196616 | tf_op jit(solution)/shard_map/while/body/eval_jaxpr/ppermute | solution.py:18
  269.2 8.7 %collective-permute-start.3 = (bf16[256,128]{1,0:T(8,128)(2,1)S(1)}, bf16[256,128]{1,0:T(8,128)(2,1)S(1)}, u32[]{:S(2)}, u32[]{:S(2)}) collective-permute-start(bf16[256,128]{1,0:T(8,128)(2,1)S(1)} %get-tuple-element.737), channel_id=1, source_target_pairs={{0,16},{16,32},{32,48},{48,64},{64,80},{80,96},{96,112},{112,128},... | collective-permute-start | bytes 196616 | tf_op jit(solution)/shard_map/while/body/eval_jaxpr/ppermute | solution.py:18
  280.1 8.3 %collective-permute-start.2 = (bf16[256,128]{1,0:T(8,128)(2,1)S(1)}, bf16[256,128]{1,0:T(8,128)(2,1)S(1)}, u32[]{:S(2)}, u32[]{:S(2)}) collective-permute-start(bf16[256,128]{1,0:T(8,128)(2,1)S(1)} %get-tuple-element.736), channel_id=1, source_target_pairs={{0,16},{16,32},{32,48},{48,64},{64,80},{80,96},{96,112},{112,128},... | collective-permute-start | bytes 196616 | tf_op jit(solution)/shard_map/while/body/eval_jaxpr/ppermute | solution.py:18
  282.1 8.3 %collective-permute-start.3 = (bf16[256,128]{1,0:T(8,128)(2,1)S(1)}, bf16[256,128]{1,0:T(8,128)(2,1)S(1)}, u32[]{:S(2)}, u32[]{:S(2)}) collective-permute-start(bf16[256,128]{1,0:T(8,128)(2,1)S(1)} %get-tuple-element.737), channel_id=1, source_target_pairs={{0,16},{16,32},{32,48},{48,64},{64,80},{80,96},{96,112},{112,128},... | collective-permute-start | bytes 196616 | tf_op jit(solution)/shard_map/while/body/eval_jaxpr/ppermute | solution.py:18
  292.5 8.3 %collective-permute-start.2 = (bf16[256,128]{1,0:T(8,128)(2,1)S(1)}, bf16[256,128]{1,0:T(8,128)(2,1)S(1)}, u32[]{:S(2)}, u32[]{:S(2)}) collective-permute-start(bf16[256,128]{1,0:T(8,128)(2,1)S(1)} %get-tuple-element.736), channel_id=1, source_target_pairs={{0,16},{16,32},{32,48},{48,64},{64,80},{80,96},{96,112},{112,128},... | collective-permute-start | bytes 196616 | tf_op jit(solution)/shard_map/while/body/eval_jaxpr/ppermute | solution.py:18
  294.5 8.3 %collective-permute-start.3 = (bf16[256,128]{1,0:T(8,128)(2,1)S(1)}, bf16[256,128]{1,0:T(8,128)(2,1)S(1)}, u32[]{:S(2)}, u32[]{:S(2)}) collective-permute-start(bf16[256,128]{1,0:T(8,128)(2,1)S(1)} %get-tuple-element.737), channel_id=1, source_target_pairs={{0,16},{16,32},{32,48},{48,64},{64,80},{80,96},{96,112},{112,128},... | collective-permute-start | bytes 196616 | tf_op jit(solution)/shard_map/while/body/eval_jaxpr/ppermute | solution.py:18
  306.0 6.9 %collective-permute-start.1 = (f32[256,128]{1,0:T(8,128)S(1)}, f32[256,128]{1,0:T(8,128)S(1)}, u32[]{:S(2)}, u32[]{:S(2)}) collective-permute-start(f32[256,128]{1,0:T(8,128)S(1)} %get-tuple-element.784), channel_id=1, source_target_pairs={{16,0},{32,16},{48,32},{64,48},{80,64},{96,80},{112,96},{128,112},... | collective-permute-start | bytes 393224 | tf_op jit(solution)/shard_map/while/body/eval_jaxpr/ppermute | solution.py:18
  309.9 7.8 %collective-permute-start = (f32[256,128]{1,0:T(8,128)S(1)}, f32[256,128]{1,0:T(8,128)S(1)}, u32[]{:S(2)}, u32[]{:S(2)}) collective-permute-start(f32[256,128]{1,0:T(8,128)S(1)} %get-tuple-element.783), channel_id=1, source_target_pairs={{16,0},{32,16},{48,32},{64,48},{80,64},{96,80},{112,96},{128,112},... | collective-permute-start | bytes 393224 | tf_op jit(solution)/shard_map/while/body/eval_jaxpr/ppermute | solution.py:18
  318.6 6.9 %collective-permute-start.1 = (f32[256,128]{1,0:T(8,128)S(1)}, f32[256,128]{1,0:T(8,128)S(1)}, u32[]{:S(2)}, u32[]{:S(2)}) collective-permute-start(f32[256,128]{1,0:T(8,128)S(1)} %get-tuple-element.784), channel_id=1, source_target_pairs={{16,0},{32,16},{48,32},{64,48},{80,64},{96,80},{112,96},{128,112},... | collective-permute-start | bytes 393224 | tf_op jit(solution)/shard_map/while/body/eval_jaxpr/ppermute | solution.py:18
  321.7 6.9 %collective-permute-start = (f32[256,128]{1,0:T(8,128)S(1)}, f32[256,128]{1,0:T(8,128)S(1)}, u32[]{:S(2)}, u32[]{:S(2)}) collective-permute-start(f32[256,128]{1,0:T(8,128)S(1)} %get-tuple-element.783), channel_id=1, source_target_pairs={{16,0},{32,16},{48,32},{64,48},{80,64},{96,80},{112,96},{128,112},... | collective-permute-start | bytes 393224 | tf_op jit(solution)/shard_map/while/body/eval_jaxpr/ppermute | solution.py:18
  329.5 7.6 %collective-permute-start.1 = (f32[256,128]{1,0:T(8,128)S(1)}, f32[256,128]{1,0:T(8,128)S(1)}, u32[]{:S(2)}, u32[]{:S(2)}) collective-permute-start(f32[256,128]{1,0:T(8,128)S(1)} %get-tuple-element.784), channel_id=1, source_target_pairs={{16,0},{32,16},{48,32},{64,48},{80,64},{96,80},{112,96},{128,112},... | collective-permute-start | bytes 393224 | tf_op jit(solution)/shard_map/while/body/eval_jaxpr/ppermute | solution.py:18
  334.3 7.6 %collective-permute-start = (f32[256,128]{1,0:T(8,128)S(1)}, f32[256,128]{1,0:T(8,128)S(1)}, u32[]{:S(2)}, u32[]{:S(2)}) collective-permute-start(f32[256,128]{1,0:T(8,128)S(1)} %get-tuple-element.783), channel_id=1, source_target_pairs={{16,0},{32,16},{48,32},{64,48},{80,64},{96,80},{112,96},{128,112},... | collective-permute-start | bytes 393224 | tf_op jit(solution)/shard_map/while/body/eval_jaxpr/ppermute | solution.py:18
  342.8 8.5 %collective-permute-start.1 = (f32[256,128]{1,0:T(8,128)S(1)}, f32[256,128]{1,0:T(8,128)S(1)}, u32[]{:S(2)}, u32[]{:S(2)}) collective-permute-start(f32[256,128]{1,0:T(8,128)S(1)} %get-tuple-element.784), channel_id=1, source_target_pairs={{16,0},{32,16},{48,32},{64,48},{80,64},{96,80},{112,96},{128,112},... | collective-permute-start | bytes 393224 | tf_op jit(solution)/shard_map/while/body/eval_jaxpr/ppermute | solution.py:18
  347.5 7.7 %collective-permute-start = (f32[256,128]{1,0:T(8,128)S(1)}, f32[256,128]{1,0:T(8,128)S(1)}, u32[]{:S(2)}, u32[]{:S(2)}) collective-permute-start(f32[256,128]{1,0:T(8,128)S(1)} %get-tuple-element.783), channel_id=1, source_target_pairs={{16,0},{32,16},{48,32},{64,48},{80,64},{96,80},{112,96},{128,112},... | collective-permute-start | bytes 393224 | tf_op jit(solution)/shard_map/while/body/eval_jaxpr/ppermute | solution.py:18
  356.2 8.9 %collective-permute-start.1 = (f32[256,128]{1,0:T(8,128)S(1)}, f32[256,128]{1,0:T(8,128)S(1)}, u32[]{:S(2)}, u32[]{:S(2)}) collective-permute-start(f32[256,128]{1,0:T(8,128)S(1)} %get-tuple-element.784), channel_id=1, source_target_pairs={{16,0},{32,16},{48,32},{64,48},{80,64},{96,80},{112,96},{128,112},... | collective-permute-start | bytes 393224 | tf_op jit(solution)/shard_map/while/body/eval_jaxpr/ppermute | solution.py:18
  361.4 6.9 %collective-permute-start = (f32[256,128]{1,0:T(8,128)S(1)}, f32[256,128]{1,0:T(8,128)S(1)}, u32[]{:S(2)}, u32[]{:S(2)}) collective-permute-start(f32[256,128]{1,0:T(8,128)S(1)} %get-tuple-element.783), channel_id=1, source_target_pairs={{16,0},{32,16},{48,32},{64,48},{80,64},{96,80},{112,96},{128,112},... | collective-permute-start | bytes 393224 | tf_op jit(solution)/shard_map/while/body/eval_jaxpr/ppermute | solution.py:18
  369.2 8.9 %collective-permute-start.1 = (f32[256,128]{1,0:T(8,128)S(1)}, f32[256,128]{1,0:T(8,128)S(1)}, u32[]{:S(2)}, u32[]{:S(2)}) collective-permute-start(f32[256,128]{1,0:T(8,128)S(1)} %get-tuple-element.784), channel_id=1, source_target_pairs={{16,0},{32,16},{48,32},{64,48},{80,64},{96,80},{112,96},{128,112},... | collective-permute-start | bytes 393224 | tf_op jit(solution)/shard_map/while/body/eval_jaxpr/ppermute | solution.py:18
  382.2 8.6 %collective-permute-start.1 = (f32[256,128]{1,0:T(8,128)S(1)}, f32[256,128]{1,0:T(8,128)S(1)}, u32[]{:S(2)}, u32[]{:S(2)}) collective-permute-start(f32[256,128]{1,0:T(8,128)S(1)} %get-tuple-element.784), channel_id=1, source_target_pairs={{16,0},{32,16},{48,32},{64,48},{80,64},{96,80},{112,96},{128,112},... | collective-permute-start | bytes 393224 | tf_op jit(solution)/shard_map/while/body/eval_jaxpr/ppermute | solution.py:18
  394.9 8.1 %collective-permute-start.1 = (f32[256,128]{1,0:T(8,128)S(1)}, f32[256,128]{1,0:T(8,128)S(1)}, u32[]{:S(2)}, u32[]{:S(2)}) collective-permute-start(f32[256,128]{1,0:T(8,128)S(1)} %get-tuple-element.784), channel_id=1, source_target_pairs={{16,0},{32,16},{48,32},{64,48},{80,64},{96,80},{112,96},{128,112},... | collective-permute-start | bytes 393224 | tf_op jit(solution)/shard_map/while/body/eval_jaxpr/ppermute | solution.py:18
  407.4 7.5 %collective-permute-start.1 = (f32[256,128]{1,0:T(8,128)S(1)}, f32[256,128]{1,0:T(8,128)S(1)}, u32[]{:S(2)}, u32[]{:S(2)}) collective-permute-start(f32[256,128]{1,0:T(8,128)S(1)} %get-tuple-element.784), channel_id=1, source_target_pairs={{16,0},{32,16},{48,32},{64,48},{80,64},{96,80},{112,96},{128,112},... | collective-permute-start | bytes 393224 | tf_op jit(solution)/shard_map/while/body/eval_jaxpr/ppermute | solution.py:18
  419.7 7.4 %collective-permute-start.1 = (f32[256,128]{1,0:T(8,128)S(1)}, f32[256,128]{1,0:T(8,128)S(1)}, u32[]{:S(2)}, u32[]{:S(2)}) collective-permute-start(f32[256,128]{1,0:T(8,128)S(1)} %get-tuple-element.784), channel_id=1, source_target_pairs={{16,0},{32,16},{48,32},{64,48},{80,64},{96,80},{112,96},{128,112},... | collective-permute-start | bytes 393224 | tf_op jit(solution)/shard_map/while/body/eval_jaxpr/ppermute | solution.py:18
  431.6 8.0 %collective-permute-start.1 = (f32[256,128]{1,0:T(8,128)S(1)}, f32[256,128]{1,0:T(8,128)S(1)}, u32[]{:S(2)}, u32[]{:S(2)}) collective-permute-start(f32[256,128]{1,0:T(8,128)S(1)} %get-tuple-element.784), channel_id=1, source_target_pairs={{16,0},{32,16},{48,32},{64,48},{80,64},{96,80},{112,96},{128,112},... | collective-permute-start | bytes 393224 | tf_op jit(solution)/shard_map/while/body/eval_jaxpr/ppermute | solution.py:18
  443.4 7.3 %collective-permute-start.1 = (f32[256,128]{1,0:T(8,128)S(1)}, f32[256,128]{1,0:T(8,128)S(1)}, u32[]{:S(2)}, u32[]{:S(2)}) collective-permute-start(f32[256,128]{1,0:T(8,128)S(1)} %get-tuple-element.784), channel_id=1, source_target_pairs={{16,0},{32,16},{48,32},{64,48},{80,64},{96,80},{112,96},{128,112},... | collective-permute-start | bytes 393224 | tf_op jit(solution)/shard_map/while/body/eval_jaxpr/ppermute | solution.py:18
  (17 other events, 120.6 us)
Sparse Core Ops, SparseCore 0:
  10.4 71.1 all-gather.1
where the time goes:
time: 502 us; the launch traced here: 500 us
  waiting for transfers between devices  195 us (39%)
  starting transfers between devices  152 us (30%)
  matrix products  74.6 us (15%)
  other arithmetic  49.8 us (10%)
  between operations  14.2 us (3%)
  local copies, waits for them, and re-layouts  11.3 us (2%)
    ppermute x60, starting transfers between devices, passed_along(): return lax.ppermute(shard, axis, pairs)  152 us
    ppermute x60, waiting for transfers between devices, passed_along(): return lax.ppermute(shard, axis, pairs)  130 us
    all_gather x1, waiting for transfers between devices, local(): key_rows = lax.all_gather(keys, 'ctx', axis=0, tiled=True)  65.8 us
    dot_general x16, matrix products, grad_step(): jnp.einsum('hqk,qhe->ke', dscore_round, query_three, preferred_element_ty...  16.7 us
    dot_general x16, matrix products, grad_step(): jnp.einsum('hqk,qhe->ke', weights_round, grad_three, preferred_element_ty...  16.7 us
    reduce_sum x1, other arithmetic, local(): jnp.sum(jnp.where(allowed[None], jnp.exp(masked - new_max), 0.0), axis=-1...  14.9 us
    dot_general x1, matrix products, local(): jnp.einsum('qhe,ke->hqk', query_three, key_rows, preferred_element_type=j...  14.7 us
    add x15, other arithmetic, return_turn(): key_sum + lax.dynamic_index_in_dim(key_store, section, 0, keepdims=False)  13.9 us
  transfers between devices with their start and end apart: 61, of which 59 were waited for; matrix products, arithmetic and copies ran while one was open for 10% of the time, Pallas kernels for 0%

commit v1 on v0

v1 whole, which is shorter than its diff:
```python
import math

import jax
import jax.numpy as jnp
from jax import lax
from jax.experimental import pallas as pl
from jax.experimental.pallas import tpu as pltpu
from jax.sharding import PartitionSpec as P

HEADS = 8
HEAD = 128
ROWS = 256
WIDE = HEADS * ROWS
RING = 8
SCALE = 1.0 / math.sqrt(HEAD)
LOG2_SCALE = SCALE * math.log2(math.e)
BIG = float(2.0**100)
OWN = 3
REACH = 12

ORDER = (
    (1, -4), (1, 3), (1, 1),
    (1, -3), (0, 4), (1, 2),
    (0, -3), (0, 3), (1, -2),
    (0, -2), (0, 2), (1, -1),
    (0, -1), (0, 1), (1, 0),
)


def slot_id(r, d):
    return d + 3 if r == 0 else d + 12


SLOTS = tuple(slot_id(r, d) for r, d in ORDER)


def dot(a, b):
    return lax.dot_general(a, b, (((1,), (0,)), ((), ())), preferred_element_type=jnp.float32)


def pick(index, values):
    out = jnp.int32(values[0])
    for i in range(1, len(values)):
        out = jnp.where(index == i, jnp.int32(values[i]), out)
    return out


def children(r, d):
    found = []
    if r == 0:
        if -3 < d <= 0:
            found.append(("up", None, (0, d - 1)))
        if 0 <= d < 4:
            found.append(("down", None, (0, d + 1)))
        if -2 <= d <= 2:
            found.append(("across", 0, (1, d)))
    else:
        if d in (-2, -3):
            found.append(("up", 1, (1, d - 1)))
        if d == 2:
            found.append(("down", 1, (1, 3)))
    return found


def kernel(
    docs, q, k, v, o, do, dq, dk, dv,
    qt, dot_, qb, dob, kall, vall, ebuf, seen, top, total, lse, dqt, pbuf, dsbuf, acck, accv, sendk, sendv, landk, landv,
    kgs, kgr, vgs, vgr, krs, krr, vrs, vrr,
):
    me = lax.axis_index("ctx")
    row = me // RING
    z = me % RING
    up = row * RING + (z + 1) % RING
    down = row * RING + (z + RING - 1) % RING
    across = (1 - row) * RING + z
    where = {"up": up, "down": down, "across": across}

    barrier = pltpu.get_barrier_semaphore()
    for other in (up, down, across):
        pl.semaphore_signal(barrier, inc=1, device_id={"ctx": other}, device_id_type=pl.DeviceIdType.MESH)

    kall[OWN] = k[...]
    vall[OWN] = v[...]
    pl.semaphore_wait(barrier, 3)

    def remote(src, dst, ssem, rsem, target):
        return pltpu.make_async_remote_copy(
            src_ref=src, dst_ref=dst, send_sem=ssem, recv_sem=rsem,
            device_id={"ctx": target}, device_id_type=pl.DeviceIdType.MESH,
        )

    gathers = ((kall, kgs, kgr), (vall, vgs, vgr))

    def only(need_row, action):
        if need_row is None:
            action()
        else:
            pl.when(row == need_row)(action)

    def forward(which, r, d):
        buf, ssem, rsem = gathers[which]
        s = slot_id(r, d)
        for direction, need_row, there in children(r, d):
            t = slot_id(*there)

            def go(direction=direction, t=t):
                remote(buf.at[s], buf.at[t], ssem.at[t], rsem.at[t], where[direction]).start()

            only(need_row, go)

    def arrived(which, r, d):
        buf, ssem, rsem = gathers[which]
        s = slot_id(r, d)

        def go():
            remote(buf.at[s], buf.at[s], ssem.at[s], rsem.at[s], up).wait_recv()

        only(None if r == 0 else 1, go)

    forward(0, 0, 0)
    forward(1, 0, 0)

    row16 = lax.broadcasted_iota(jnp.int32, (16, ROWS), 0)
    lane = lax.broadcasted_iota(jnp.int32, (ROWS, HEAD), 1)
    rowk = lax.broadcasted_iota(jnp.int32, (ROWS, HEAD), 0)
    qdoc = jnp.where(lax.broadcasted_iota(jnp.int32, (16, ROWS), 1) < 128, docs[2 * me], docs[2 * me + 1])
    mask_rows = jnp.where((row16 < 8) & (row16 != qdoc), -BIG, 0.0).astype(jnp.bfloat16)
    zeros = jnp.zeros((112, ROWS), jnp.bfloat16)
    for h in range(HEADS):
        sl = slice(h * ROWS, (h + 1) * ROWS)
        cols = slice(h * HEAD, (h + 1) * HEAD)
        qh, dh = q[:, cols], do[:, cols]
        qb[sl, :] = qh
        dob[sl, :] = dh
        qt[:HEAD, sl] = qh.T
        qt[HEAD : HEAD + 16, sl] = mask_rows
        qt[HEAD + 16 :, sl] = zeros
        dot_[:HEAD, sl] = dh.T
        prod = dh.astype(jnp.float32) * o[:, cols].astype(jnp.float32)
        minus = -jnp.sum(prod.T, axis=0, keepdims=True)
        hi = minus.astype(jnp.bfloat16).astype(jnp.float32)
        mid = (minus - hi).astype(jnp.bfloat16).astype(jnp.float32)
        low = minus - hi - mid
        rows = jnp.where(row16 == 0, hi, jnp.where(row16 == 1, mid, jnp.where(row16 == 2, low, 0.0)))
        dot_[HEAD : HEAD + 16, sl] = rows.astype(jnp.bfloat16)
        dot_[HEAD + 16 :, sl] = zeros
    dqt[...] = jnp.zeros_like(dqt)
    landk[OWN] = jnp.zeros((ROWS, HEAD), jnp.bfloat16)
    landv[OWN] = jnp.zeros((ROWS, HEAD), jnp.bfloat16)

    def block_of(s):
        far = s >= 8
        d = jnp.where(far, s - 12, s - 3)
        brow = jnp.where(far, 1 - row, row)
        return brow * RING + (z + d + RING) % RING

    def needed(s):
        b = block_of(s)
        return ((s < 8) | (row == 1)) & (b < me) & (b >= me - REACH)

    def first_pass(s, own):
        b = me if own else block_of(s)
        kdoc = jnp.where(rowk < 128, docs[2 * b], docs[2 * b + 1])
        hot = jnp.where(lane == kdoc, 1.0, 0.0).astype(jnp.bfloat16)
        ka = jnp.concatenate([kall[s], hot], axis=1)
        for h in range(HEADS):
            sl = slice(h * ROWS, (h + 1) * ROWS)
            score = dot(ka, qt[:, sl])
            if own:
                keep = lax.broadcasted_iota(jnp.int32, (ROWS, ROWS), 0) <= lax.broadcasted_iota(
                    jnp.int32, (ROWS, ROWS), 1
                )
                score = jnp.where(keep, score, -BIG)
            score = score.reshape(ROWS // 8, 8, ROWS)
            new = jnp.max(score, axis=0)
            if not own:
                old = top[:, sl]
                new = jnp.maximum(old, new)
            e = jnp.exp2((score - new[None]) * LOG2_SCALE)
            added = jnp.sum(e, axis=0)
            if not own:
                added = added + total[:, sl] * jnp.exp2((old - new) * LOG2_SCALE)
            total[:, sl] = added
            top[:, sl] = new
            seen[s, :, sl] = new
            ebuf[s, h] = e.reshape(ROWS, ROWS)

    first_pass(OWN, True)

    @pl.loop(0, 15)
    def _(step):
        for group in range(5):
            @pl.when(step == 3 * group)
            def _():
                for r, d in ORDER[12 - 3 * group : 15 - 3 * group]:
                    arrived(0, r, d)
                    forward(0, r, d)
                if group >= 1:
                    for r, d in ORDER[15 - 3 * group : 18 - 3 * group]:
                        arrived(1, r, d)
                        forward(1, r, d)

        s = pick(14 - step, SLOTS)

        @pl.when(needed(s))
        def _():
            first_pass(s, False)

    for r, d in ORDER[0:3]:
        arrived(1, r, d)

    peak = jnp.max(top[...], axis=0, keepdims=True)
    norm = jnp.sum(total[...] * jnp.exp2((top[...] - peak) * LOG2_SCALE), axis=0, keepdims=True)
    top[...] = jnp.broadcast_to(peak, (8, WIDE))
    lse[...] = jnp.broadcast_to(jnp.log2(norm), (8, WIDE))

    ones = jnp.where(lane < 3, 1.0, 0.0).astype(jnp.bfloat16)

    def stage_a(s, half):
        va = jnp.concatenate([vall[s], ones], axis=1)
        for h in range(HEADS):
            sl = slice(h * ROWS, (h + 1) * ROWS)
            inner = dot(va, dot_[:, sl])
            factor = jnp.exp2((seen[s, :, sl] - top[:, sl]) * LOG2_SCALE - lse[:, sl])
            prob = (ebuf[s, h].reshape(ROWS // 8, 8, ROWS) * factor[None]).reshape(ROWS, ROWS)
            pbuf[half, :, sl] = prob.astype(jnp.bfloat16)
            dsbuf[half, :, sl] = (prob * inner).astype(jnp.bfloat16)

    def stage_b(s, half):
        accv[...] = dot(pbuf[half], dob[...])
        acck[...] = dot(dsbuf[half], qb[...])
        dqt[...] += dot(kall[s].T, dsbuf[half])

    def following(step):
        out = jnp.int32(OWN)
        for i in reversed(range(15)):
            s = SLOTS[i]
            out = jnp.where((step < i) & needed(jnp.int32(s)), jnp.int32(s), out)
        return out

    returns = ((vall, accv, sendv, landv, vrs, vrr), (kall, acck, sendk, landk, krs, krr))

    stage_a(following(jnp.int32(-1)), 0)

    def returning(step, half):
        s = pick(step, SLOTS)
        far = s >= 8
        d = jnp.where(far, s - 12, s - 3)
        use = needed(s)

        @pl.when(use)
        def _():
            stage_a(following(step), 1 - half)
            stage_b(s, half)

        @pl.when(jnp.logical_not(use))
        def _():
            acck[...] = jnp.zeros_like(acck)
            accv[...] = jnp.zeros_like(accv)

        size = jnp.where(d < 0, -d, d)
        has_z = jnp.where(far, (d == -3) | (d == -2) | (d == 2), (d > -3) & (d < 4))
        has_y = (row == 0) & jnp.logical_not(far) & (size <= 2)
        z_from = jnp.where(has_z, jnp.where(d < 0, s - 1, s + 1), OWN)
        y_from = jnp.where(has_y, s + 9, OWN)
        target = jnp.where(far & (size <= 2), across, jnp.where(d < 0, down, up))

        @pl.when((row == 1) | jnp.logical_not(far))
        def _():
            for _, acc, out, land, ssem, rsem in returns:
                @pl.when(has_z)
                def _():
                    remote(land.at[z_from], land.at[z_from], ssem.at[z_from], rsem.at[z_from], up).wait_recv()

                @pl.when(has_y)
                def _():
                    remote(land.at[y_from], land.at[y_from], ssem.at[y_from], rsem.at[y_from], up).wait_recv()

                out[s] = (
                    acc[...] + land[z_from].astype(jnp.float32) + land[y_from].astype(jnp.float32)
                ).astype(jnp.bfloat16)
                remote(out.at[s], land.at[s], ssem.at[s], rsem.at[s], target).start()

        return jnp.where(use, 1 - half, half)

    half = lax.fori_loop(0, 15, returning, jnp.int32(0))
    stage_b(OWN, half)

    for h in range(HEADS):
        dq[:, h * HEAD : (h + 1) * HEAD] = (dqt[:, h * ROWS : (h + 1) * ROWS].T * SCALE).astype(jnp.bfloat16)

    y_from = jnp.where(row == 0, slot_id(1, 0), OWN)
    for (_, acc, out, land, ssem, rsem), result, factor in zip(returns, (dv, dk), (None, SCALE)):
        for s in (slot_id(0, -1), slot_id(0, 1)):
            remote(land.at[s], land.at[s], ssem.at[s], rsem.at[s], up).wait_recv()

        @pl.when(row == 0)
        def _():
            s = slot_id(1, 0)
            remote(land.at[s], land.at[s], ssem.at[s], rsem.at[s], up).wait_recv()

        whole = acc[...]
        for s in (slot_id(0, -1), slot_id(0, 1), y_from):
            whole = whole + land[s].astype(jnp.float32)
        if factor is not None:
            whole = whole * factor
        result[...] = whole.astype(jnp.bfloat16)

    for r, d in ORDER + ((0, 0),):
        for which in range(2):
            buf, ssem, rsem = gathers[which]
            for direction, need_row, there in children(r, d):
                t = slot_id(*there)

                def go(t=t):
                    remote(buf.at[t], buf.at[t], ssem.at[t], rsem.at[t], up).wait_send()

                only(need_row, go)
    for r, d in ORDER:
        s = slot_id(r, d)
        for _, acc, out, land, ssem, rsem in returns:

            def go():
                remote(out.at[s], land.at[s], ssem.at[s], rsem.at[s], up).wait_send()

            only(None if r == 0 else 1, go)


def local(queries, keys, values, attn_out, out_grad, tile_doc):
    vmem = pl.BlockSpec(memory_space=pltpu.VMEM)
    bf16, f32 = jnp.bfloat16, jnp.float32
    return pl.pallas_call(
        kernel,
        out_shape=(
            jax.ShapeDtypeStruct((ROWS, HEADS * HEAD), bf16),
            jax.ShapeDtypeStruct((ROWS, HEAD), bf16),
            jax.ShapeDtypeStruct((ROWS, HEAD), bf16),
        ),
        in_specs=[pl.BlockSpec(memory_space=pltpu.SMEM)] + [vmem] * 5,
        out_specs=(vmem, vmem, vmem),
        scratch_shapes=[
            pltpu.VMEM((2 * HEAD, WIDE), bf16),
            pltpu.VMEM((2 * HEAD, WIDE), bf16),
            pltpu.VMEM((WIDE, HEAD), bf16),
            pltpu.VMEM((WIDE, HEAD), bf16),
            pltpu.VMEM((16, ROWS, HEAD), bf16),
            pltpu.VMEM((16, ROWS, HEAD), bf16),
            pltpu.VMEM((16, HEADS, ROWS, ROWS), f32),
            pltpu.VMEM((16, 8, WIDE), f32),
            pltpu.VMEM((8, WIDE), f32),
            pltpu.VMEM((8, WIDE), f32),
            pltpu.VMEM((8, WIDE), f32),
            pltpu.VMEM((HEAD, WIDE), f32),
            pltpu.VMEM((2, ROWS, WIDE), bf16),
            pltpu.VMEM((2, ROWS, WIDE), bf16),
            pltpu.VMEM((ROWS, HEAD), f32),
            pltpu.VMEM((ROWS, HEAD), f32),
            pltpu.VMEM((16, ROWS, HEAD), bf16),
            pltpu.VMEM((16, ROWS, HEAD), bf16),
            pltpu.VMEM((16, ROWS, HEAD), bf16),
            pltpu.VMEM((16, ROWS, HEAD), bf16),
        ]
        + [pltpu.SemaphoreType.DMA((16,))] * 8,
        compiler_params=pltpu.CompilerParams(
            collective_id=0, has_side_effects=True, vmem_limit_bytes=60 * 2**20
        ),
        name="attention_backward",
    )(tile_doc, queries, keys, values, attn_out, out_grad)


def solution(mesh):
    rows = P(("seq", "ctx"), None)
    return jax.shard_map(
        local,
        mesh=mesh,
        in_specs=(rows, rows, rows, rows, rows, P("seq")),
        out_specs=(rows, rows, rows),
        check_vma=False,
    )
```

time: 502 us -> 67.6 us (0.13)
  the two profiles are of different devices: /device:TPU:8 before, /device:TPU:6 now
where the time goes in v1:
time: 67.6 us; the launch traced here: 67.5 us
  Pallas kernels  63.4 us (94%)
  local copies, waits for them, and re-layouts  3.4 us (5%)
    pallas_call x1, Pallas kernels, local(): pl.pallas_call(kernel, out_shape=(jax.ShapeDtypeStruct((ROWS, HEADS * HEA...  63.4 us
    unnamed x7, local copies, waits for them, and re-layouts  3.4 us

profile of v1, /device:TPU:6, one launch (start us, length us, event | category | flops | bytes accessed | tf_op | source)
XLA Modules:
  0.0 67.5 jit_solution(3080666056054301880)
XLA Ops:
  0.6 63.4 %attention_backward.1 = (bf16[256,1024]{1,0:T(8,128)(2,1)}, bf16[256,128]{1,0:T(8,128)(2,1)}, bf16[256,128]{1,0:T(8,128)(2,1)}) custom-call(s32[32]{0:T(128)} %docs.1, bf16[256,1024]{1,0:T(8,128)(2,1)} %q.1, bf16[256,128]{1,0:T(8,128)(2,1)} %k.1, bf16[256,128]{1,0:T(8,128)(2,1)} %v.1, bf16[256,1024]{1,0:T(8,128)(2,1)} %o.1, bf16[256,1024]{1,0:T(8,128)(2,1)} %do.1), custom_call_target="tpu_custom_call" | custom-call | tf_op jit(solution)/shard_map/attention_backward/pallas_call | solution.py:332
  64.0 0.0 copy-start.1
  64.1 1.9 %copy.12 = bf16[256,1024]{1,0:T(8,128)(2,1)} copy(bf16[256,1024]{1,0:T(8,128)(2,1)} %get-tuple-element.6) | data formatting | bytes 1048576
  66.0 0.0 copy-done.1
  66.0 0.0 copy-start
  66.0 0.6 copy.13
  66.6 0.2 copy-done
  66.8 0.6 copy.14
Async XLA Ops:
  64.0 1.9 %copy-start.1 = (bf16[256,128]{1,0:T(8,128)(2,1)S(1)}, bf16[256,128]{1,0:T(8,128)(2,1)}, u32[]{:S(2)}) copy-start(bf16[256,128]{1,0:T(8,128)(2,1)} %get-tuple-element.7) | copy-start | bytes 196612
  66.0 0.9 %copy-start = (bf16[256,128]{1,0:T(8,128)(2,1)S(1)}, bf16[256,128]{1,0:T(8,128)(2,1)}, u32[]{:S(2)}) copy-start(bf16[256,128]{1,0:T(8,128)(2,1)} %get-tuple-element.8) | copy-start | bytes 196612

commit v2 on v1

v2 whole, which is shorter than its diff:
```python
import math

import jax
import jax.numpy as jnp
from jax import lax
from jax.experimental import pallas as pl
from jax.experimental.pallas import tpu as pltpu
from jax.sharding import PartitionSpec as P

HEADS = 8
HEAD = 128
ROWS = 256
WIDE = HEADS * ROWS
RING = 8
SCALE = 1.0 / math.sqrt(HEAD)
LOG2_SCALE = SCALE * math.log2(math.e)
BIG = float(2.0**100)
OWN = 3
REACH = 12

ORDER = (
    (0, -1), (1, 0), (0, 1), (0, -2), (0, 2),
    (1, -1), (1, 1), (1, -2), (1, 2),
    (0, -3), (0, 3), (1, -3), (1, 3),
    (0, 4), (1, 4),
)
BACK = (
    (1, 0), (0, -1), (0, 1), (1, -1),
    (1, 4), (0, 4), (1, 3), (1, -3), (0, 3), (0, -3), (1, 2), (1, -2), (1, 1), (0, 2), (0, -2),
)
SENDS = tuple([(3, (1, -1))] + [(n, BACK[n]) for n in range(4, 15)] + [(14, x) for x in BACK[:3]])
BOTH, ROW0, ROW1 = (0, 1), (0,), (1,)
ARRIVALS = (
    ((ROW0, (0, -2)), (ROW0, (0, 2)), (BOTH, (0, -1)), (BOTH, (0, 1)), (ROW1, (1, 0))),
    ((ROW1, (1, -2)), (ROW1, (1, 2)), (BOTH, (0, -3), 0), (BOTH, (0, 3), 0), (ROW1, (0, -2)), (ROW1, (0, 2)),
     (ROW1, (1, -1)), (ROW1, (1, 1))),
    ((ROW1, (1, -3)), (ROW1, (1, 3)), (ROW1, (0, -3)), (ROW1, (0, 3)), (ROW0, (0, 4))),
    ((ROW1, (0, 4)), (ROW1, (1, 4))),
)
KEY_STEPS = (0, 3, 9, 13)
VALUE_STEPS = (5, 10, 14, None)
LAST_VALUES = 2


def slot_id(r, d):
    return d + 3 if r == 0 else d + 11


SLOTS = tuple(slot_id(r, d) for r, d in ORDER)

RAW_EDGES = (
    ((0, -1), (0, 0), 1, 0, lambda r, z: True),
    ((0, -2), (0, 0), 2, 0, lambda r, z: r == 0),
    ((0, 1), (0, 0), -1, 0, lambda r, z: True),
    ((0, 2), (0, 0), -2, 0, lambda r, z: r == 0),
    ((1, 0), (0, 0), 0, 1, lambda r, z: r == 1),
    ((0, -2), (0, -1), 1, 0, lambda r, z: r == 1),
    ((0, 2), (0, 1), -1, 0, lambda r, z: r == 1),
    ((1, -2), (0, -2), 0, 1, lambda r, z: r == 1),
    ((1, 2), (0, 2), 0, 1, lambda r, z: r == 1),
    ((1, -1), (0, -1), 0, 1, lambda r, z: r == 1),
    ((1, 1), (1, 0), -1, 0, lambda r, z: r == 1),
    ((0, -3), (0, -2), 1, 0, lambda r, z: True),
    ((0, 3), (0, 2), -1, 0, lambda r, z: True),
    ((1, -3), (0, -3), 0, 1, lambda r, z: r == 1 and z >= 3),
    ((1, -3), (1, -2), 1, 0, lambda r, z: r == 1 and z < 3),
    ((1, 3), (1, 2), -1, 0, lambda r, z: r == 1),
    ((0, 4), (0, -3), 1, 0, lambda r, z: True),
    ((1, 4), (1, -3), 1, 0, lambda r, z: r == 1 and 4 <= z < 7),
    ((1, 4), (0, 4), 0, 1, lambda r, z: r == 1 and z == 7),
    ((1, 4), (1, 3), -1, 0, lambda r, z: r == 1 and z < 4),
)


def plan():
    masks = [0] * len(RAW_EDGES)
    todo = []
    for me in range(2 * RING):
        row, z = divmod(me, RING)
        for r, d in ORDER:
            block = (row if r == 0 else 1 - row) * RING + (z + d) % RING
            if me - REACH <= block < me:
                todo.append((row, z, (r, d)))
    while todo:
        row, z, slot = todo.pop()
        if slot == (0, 0):
            continue
        found = [n for n, edge in enumerate(RAW_EDGES) if edge[0] == slot and edge[4](row, z)]
        assert len(found) == 1, (row, z, slot)
        bit = 1 << (row * RING + z)
        if not masks[found[0]] & bit:
            masks[found[0]] |= bit
            _, parent, dz, dy, _ = RAW_EDGES[found[0]]
            todo.append((row ^ dy, (z - dz) % RING, parent))
    return masks


MASKS = plan()
NEEDED = tuple(
    sum(
        1 << me
        for me in range(2 * RING)
        if me - REACH <= (me // RING ^ r) * RING + (me % RING + d) % RING < me
    )
    for r, d in ORDER
)
EDGES = tuple((slot_id(*t), slot_id(*p), dz, dy) for t, p, dz, dy, _ in RAW_EDGES)
NEED_MASKS = dict(zip(SLOTS, NEEDED))
SLOT_MASKS = {s: sum(m for m, e in zip(MASKS, EDGES) if e[0] == s) for s in range(16)}


def dot(a, b):
    return lax.dot_general(a, b, (((1,), (0,)), ((), ())), preferred_element_type=jnp.float32)


def pick(index, values):
    out = jnp.int32(values[0])
    for i in range(1, len(values)):
        out = jnp.where(index == i, jnp.int32(values[i]), out)
    return out


def kernel(
    docs, q_any, k, v, o_any, do_any, dq_any, dk, dv,
    q, o, do, dq, qt, dot_, qb, dob, kall, vall, ebuf, seen, top, total, lse, dqt, pbuf, dsbuf, acck, accv,
    sendk, sendv, landk, landv, kgs, kgr, vgs, vgr, krs, krr, vrs, vrr, here,
):
    me = lax.axis_index("ctx")
    row = me // RING
    z = me % RING

    def place(dz, dy):
        other = 1 - row if dy else row
        return other * RING + (z + dz + RING) % RING

    def in_mask(mask, device):
        return (jnp.int32(mask) >> device) & 1 == 1

    near = [(1, 0), (-1, 0), (2, 0), (-2, 0), (0, 1)]
    barrier = pltpu.get_barrier_semaphore()
    for dz, dy in near:
        pl.semaphore_signal(barrier, inc=1, device_id={"ctx": place(dz, dy)}, device_id_type=pl.DeviceIdType.MESH)

    loads = [
        pltpu.make_async_copy(src, dst, here.at[n])
        for n, (src, dst) in enumerate(((q_any, q), (do_any, do), (o_any, o)))
    ]
    for load in loads:
        load.start()
    kall[OWN] = k[...]
    vall[OWN] = v[...]
    pl.semaphore_wait(barrier, len(near))

    def remote(src, dst, ssem, rsem, target):
        return pltpu.make_async_remote_copy(
            src_ref=src, dst_ref=dst, send_sem=ssem, recv_sem=rsem,
            device_id={"ctx": target}, device_id_type=pl.DeviceIdType.MESH,
        )

    gathers = ((kall, kgs, kgr), (vall, vgs, vgr))

    def forward(which, s):
        buf, ssem, rsem = gathers[which]
        for n, (t, parent, dz, dy) in enumerate(EDGES):
            if parent == s and MASKS[n]:
                target = place(dz, dy)

                @pl.when(in_mask(MASKS[n], target))
                def _(n=n, t=t, target=target):
                    remote(buf.at[s], buf.at[t], ssem.at[n], rsem.at[t], target).start()

    def arrive(which, stage):
        buf, _, rsem = gathers[which]
        for rows, (r, d), *only in ARRIVALS[stage]:
            s = slot_id(r, d)
            mask = SLOT_MASKS[s] & sum(0xFF << (RING * n) for n in (only or rows))
            if mask:

                @pl.when(in_mask(mask, me))
                def _(s=s):
                    remote(buf.at[s], buf.at[s], here.at[0], rsem.at[s], me).wait_recv()
                    forward(which, s)

    forward(0, OWN)
    for load in loads:
        load.wait()

    row16 = lax.broadcasted_iota(jnp.int32, (16, ROWS), 0)
    lane = lax.broadcasted_iota(jnp.int32, (ROWS, HEAD), 1)
    rowk = lax.broadcasted_iota(jnp.int32, (ROWS, HEAD), 0)
    qdoc = jnp.where(lax.broadcasted_iota(jnp.int32, (16, ROWS), 1) < 128, docs[2 * me], docs[2 * me + 1])
    mask_rows = jnp.where((row16 < 8) & (row16 != qdoc), -BIG, 0.0).astype(jnp.bfloat16)
    zeros = jnp.zeros((112, ROWS), jnp.bfloat16)
    for h in range(HEADS):
        sl = slice(h * ROWS, (h + 1) * ROWS)
        cols = slice(h * HEAD, (h + 1) * HEAD)
        qh, dh = q[:, cols], do[:, cols]
        qb[sl, :] = qh
        dob[sl, :] = dh
        qt[:HEAD, sl] = qh.T
        qt[HEAD : HEAD + 16, sl] = mask_rows
        qt[HEAD + 16 :, sl] = zeros
        dot_[:HEAD, sl] = dh.T
        prod = dh.astype(jnp.float32) * o[:, cols].astype(jnp.float32)
        minus = -jnp.sum(prod.T, axis=0, keepdims=True)
        hi = minus.astype(jnp.bfloat16).astype(jnp.float32)
        mid = (minus - hi).astype(jnp.bfloat16).astype(jnp.float32)
        low = minus - hi - mid
        rows = jnp.where(row16 == 0, hi, jnp.where(row16 == 1, mid, jnp.where(row16 == 2, low, 0.0)))
        dot_[HEAD : HEAD + 16, sl] = rows.astype(jnp.bfloat16)
        dot_[HEAD + 16 :, sl] = zeros
    dqt[...] = jnp.zeros_like(dqt)

    def block_of(s):
        far = s >= 8
        d = jnp.where(far, s - 11, s - 3)
        brow = jnp.where(far, 1 - row, row)
        return brow * RING + (z + d + RING) % RING

    def first_pass(s, own):
        b = me if own else block_of(s)
        kdoc = jnp.where(rowk < 128, docs[2 * b], docs[2 * b + 1])
        hot = jnp.where(lane == kdoc, 1.0, 0.0).astype(jnp.bfloat16)
        ka = jnp.concatenate([kall[s], hot], axis=1)
        for h in range(HEADS):
            sl = slice(h * ROWS, (h + 1) * ROWS)
            score = dot(ka, qt[:, sl])
            if own:
                keep = lax.broadcasted_iota(jnp.int32, (ROWS, ROWS), 0) <= lax.broadcasted_iota(
                    jnp.int32, (ROWS, ROWS), 1
                )
                score = jnp.where(keep, score, -BIG)
            score = score.reshape(ROWS // 8, 8, ROWS)
            new = jnp.max(score, axis=0)
            if not own:
                old = top[:, sl]
                new = jnp.maximum(old, new)
            e = jnp.exp2((score - new[None]) * LOG2_SCALE)
            added = jnp.sum(e, axis=0)
            if not own:
                added = added + total[:, sl] * jnp.exp2((old - new) * LOG2_SCALE)
            total[:, sl] = added
            top[:, sl] = new
            seen[s, :, sl] = new
            ebuf[s, h] = e.reshape(ROWS, ROWS)

    first_pass(OWN, True)

    @pl.loop(0, 15)
    def _(step):
        for stage in range(4):
            for which, steps in ((0, KEY_STEPS), (1, VALUE_STEPS)):
                if steps[stage] is not None:

                    @pl.when(step == steps[stage])
                    def _(which=which, stage=stage):
                        arrive(which, stage)
                        if which == 0 and stage == 0:
                            forward(1, OWN)

        @pl.when(in_mask(pick(step, NEEDED), me))
        def _():
            first_pass(pick(step, SLOTS), False)

    peak = jnp.max(top[...], axis=0, keepdims=True)
    norm = jnp.sum(total[...] * jnp.exp2((top[...] - peak) * LOG2_SCALE), axis=0, keepdims=True)
    top[...] = jnp.broadcast_to(peak, (8, WIDE))
    lse[...] = jnp.broadcast_to(jnp.log2(norm), (8, WIDE))

    ones = jnp.where(lane < 3, 1.0, 0.0).astype(jnp.bfloat16)

    def stage_a(s, half):
        va = jnp.concatenate([vall[s], ones], axis=1)
        for h in range(HEADS):
            sl = slice(h * ROWS, (h + 1) * ROWS)
            inner = dot(va, dot_[:, sl])
            factor = jnp.exp2((seen[s, :, sl] - top[:, sl]) * LOG2_SCALE - lse[:, sl])
            prob = (ebuf[s, h].reshape(ROWS // 8, 8, ROWS) * factor[None]).reshape(ROWS, ROWS)
            pbuf[half, :, sl] = prob.astype(jnp.bfloat16)
            dsbuf[half, :, sl] = (prob * inner).astype(jnp.bfloat16)

    def stage_b(s, half):
        accv[s] = dot(pbuf[half], dob[...])
        acck[s] = dot(dsbuf[half], qb[...])
        dqt[...] += dot(kall[s].T, dsbuf[half])

    back = tuple(slot_id(r, d) for r, d in BACK)

    def following(step):
        out = jnp.int32(OWN)
        for i in reversed(range(15)):
            out = jnp.where((step < i) & in_mask(NEED_MASKS[back[i]], me), jnp.int32(back[i]), out)
        return out

    returns = ((accv, sendv, landv, vrs, vrr), (acck, sendk, landk, krs, krr))

    def add_children(s):
        for acc, out, land, ssem, rsem in returns:
            for n, (t, parent, dz, dy) in enumerate(EDGES):
                if parent == s and MASKS[n]:

                    @pl.when(in_mask(MASKS[n], place(dz, dy)))
                    def _(n=n):
                        remote(land.at[n], land.at[n], ssem.at[n], rsem.at[n], me).wait_recv()
                        acc[s] += land[n].astype(jnp.float32)

            if s == OWN:
                continue
            out[s] = acc[s].astype(jnp.bfloat16)
            for n, (t, parent, dz, dy) in enumerate(EDGES):
                if t == s and MASKS[n]:

                    @pl.when(in_mask(MASKS[n], me))
                    def _(n=n, dz=dz, dy=dy):
                        remote(out.at[s], land.at[n], ssem.at[n], rsem.at[n], place(-dz, dy)).start()

    for s in SLOTS:
        relay = SLOT_MASKS[s] & ~NEED_MASKS[s]
        if relay:

            @pl.when(in_mask(relay, me))
            def _(s=s):
                acck[s] = jnp.zeros((ROWS, HEAD), jnp.float32)
                accv[s] = jnp.zeros((ROWS, HEAD), jnp.float32)

    stage_a(following(jnp.int32(-1)), 0)

    def returning(step, half):
        use = in_mask(pick(step, tuple(NEED_MASKS[s] for s in back)), me)

        @pl.when(step == LAST_VALUES)
        def _():
            arrive(1, 3)

        @pl.when(use)
        def _():
            stage_a(following(step), 1 - half)
            stage_b(pick(step, back), half)

        for n, slot in SENDS:
            s = slot_id(*slot)

            @pl.when((step == n) & in_mask(SLOT_MASKS[s], me))
            def _(s=s):
                add_children(s)

        return jnp.where(use, 1 - half, half)

    half = lax.fori_loop(0, 15, returning, jnp.int32(0))
    stage_b(OWN, half)

    for h in range(HEADS):
        dq[:, h * HEAD : (h + 1) * HEAD] = (dqt[:, h * ROWS : (h + 1) * ROWS].T * SCALE).astype(jnp.bfloat16)
    store = pltpu.make_async_copy(dq, dq_any, here.at[0])
    store.start()
    add_children(OWN)
    dv[...] = accv[OWN].astype(jnp.bfloat16)
    dk[...] = (acck[OWN] * SCALE).astype(jnp.bfloat16)

    for n, (t, parent, dz, dy) in enumerate(EDGES):
        if MASKS[n]:

            @pl.when(in_mask(MASKS[n], place(dz, dy)))
            def _(n=n):
                for buf, ssem, rsem in gathers:
                    remote(buf.at[0], buf.at[0], ssem.at[n], rsem.at[0], me).wait_send()

            @pl.when(in_mask(MASKS[n], me))
            def _(n=n):
                for _, out, land, ssem, rsem in returns:
                    remote(out.at[0], land.at[n], ssem.at[n], rsem.at[n], me).wait_send()

    store.wait()


def hand_over(dq, dk, dv, dq_out, dk_out, dv_out):
    dq_out[...] = dq[...]
    dk_out[...] = dk[...]
    dv_out[...] = dv[...]


def local(queries, keys, values, attn_out, out_grad, tile_doc):
    vmem = pl.BlockSpec(memory_space=pltpu.VMEM)
    bf16, f32 = jnp.bfloat16, jnp.float32
    any_ = pl.BlockSpec(memory_space=pl.ANY)
    shapes = (
        jax.ShapeDtypeStruct((ROWS, HEADS * HEAD), bf16),
        jax.ShapeDtypeStruct((ROWS, HEAD), bf16),
        jax.ShapeDtypeStruct((ROWS, HEAD), bf16),
    )
    results = pl.pallas_call(
        kernel,
        out_shape=shapes,
        in_specs=[pl.BlockSpec(memory_space=pltpu.SMEM), any_, vmem, vmem, any_, any_],
        out_specs=(any_, vmem, vmem),
        scratch_shapes=[pltpu.VMEM((ROWS, HEADS * HEAD), bf16)] * 4
        + [
            pltpu.VMEM((2 * HEAD, WIDE), bf16),
            pltpu.VMEM((2 * HEAD, WIDE), bf16),
            pltpu.VMEM((WIDE, HEAD), bf16),
            pltpu.VMEM((WIDE, HEAD), bf16),
            pltpu.VMEM((16, ROWS, HEAD), bf16),
            pltpu.VMEM((16, ROWS, HEAD), bf16),
            pltpu.VMEM((16, HEADS, ROWS, ROWS), f32),
            pltpu.VMEM((16, 8, WIDE), f32),
            pltpu.VMEM((8, WIDE), f32),
            pltpu.VMEM((8, WIDE), f32),
            pltpu.VMEM((8, WIDE), f32),
            pltpu.VMEM((HEAD, WIDE), f32),
            pltpu.VMEM((2, ROWS, WIDE), bf16),
            pltpu.VMEM((2, ROWS, WIDE), bf16),
            pltpu.VMEM((16, ROWS, HEAD), f32),
            pltpu.VMEM((16, ROWS, HEAD), f32),
            pltpu.VMEM((16, ROWS, HEAD), bf16),
            pltpu.VMEM((16, ROWS, HEAD), bf16),
            pltpu.VMEM((len(EDGES), ROWS, HEAD), bf16),
            pltpu.VMEM((len(EDGES), ROWS, HEAD), bf16),
        ]
        + [pltpu.SemaphoreType.DMA((len(EDGES),))] * 8
        + [pltpu.SemaphoreType.DMA((3,))],
        compiler_params=pltpu.CompilerParams(
            collective_id=0, has_side_effects=True, vmem_limit_bytes=60 * 2**20
        ),
        name="attention_backward",
    )(tile_doc, queries, keys, values, attn_out, out_grad)
    return pl.pallas_call(
        hand_over,
        out_shape=shapes,
        in_specs=[vmem] * 3,
        out_specs=(vmem,) * 3,
        name="hand_over",
    )(*results)


def solution(mesh):
    rows = P(("seq", "ctx"), None)
    return jax.shard_map(
        local,
        mesh=mesh,
        in_specs=(rows, rows, rows, rows, rows, P("seq")),
        out_specs=(rows, rows, rows),
        check_vma=False,
    )
```

time: 67.6 us -> 62.1 us (0.919)
  the two profiles are of different devices: /device:TPU:6 before, /device:TPU:36 now
where the time goes in v2:
time: 62.1 us; the launch traced here: 61.8 us
  Pallas kernels  61.2 us (99%)
  between operations  0.64 us (1%)
    pallas_call x1, Pallas kernels, local(): pl.pallas_call(kernel, out_shape=shapes, in_specs=[pl.BlockSpec(memory_sp...  59.3 us
    pallas_call x1, Pallas kernels, local(): pl.pallas_call(hand_over, out_shape=shapes, in_specs=[vmem] * 3, out_spec...  1.92 us

profile of v2, /device:TPU:36, one launch (start us, length us, event | category | flops | bytes accessed | tf_op | source)
XLA Modules:
  0.0 61.8 jit_solution(9281376138746836130)
XLA Ops:
  0.6 59.3 %attention_backward.1 = (bf16[256,1024]{1,0:T(8,128)(2,1)}, bf16[256,128]{1,0:T(8,128)(2,1)}, bf16[256,128]{1,0:T(8,128)(2,1)}) custom-call(s32[32]{0:T(128)} %docs.1, bf16[256,1024]{1,0:T(8,128)(2,1)} %q_any.1, bf16[256,128]{1,0:T(8,128)(2,1)} %k.1, bf16[256,128]{1,0:T(8,128)(2,1)} %v.1, bf16[256,1024]{1,0:T(8,128)(2,1)} %o_any.1, bf16[256,1024]{1,0:T(8,128)(2,1)} %do_any.1), custom_call_target="tpu_custom_call" | custom-call | tf_op jit(solution)/shard_map/attention_backward/pallas_call | solution.py:391
  59.9 1.9 %hand_over.1 = (bf16[256,1024]{1,0:T(8,128)(2,1)}, bf16[256,128]{1,0:T(8,128)(2,1)}, bf16[256,128]{1,0:T(8,128)(2,1)}) custom-call(bf16[256,1024]{1,0:T(8,128)(2,1)} %get-tuple-element.6.dq, bf16[256,128]{1,0:T(8,128)(2,1)} %get-tuple-element.7.dk, bf16[256,128]{1,0:T(8,128)(2,1)} %get-tuple-element.8.dv), custom_call_target="tpu_custom_call" | custom-call | tf_op jit(solution)/shard_map/hand_over/pallas_call | solution.py:426

commit v3 on v2

--- a/solution.py
+++ b/solution.py
@@ -20,26 +20,25 @@
 
 ORDER = (
     (0, -1), (1, 0), (0, 1), (0, -2), (0, 2),
-    (1, -1), (1, 1), (1, -2), (1, 2),
-    (0, -3), (0, 3), (1, -3), (1, 3),
-    (0, 4), (1, 4),
+    (1, -1), (1, 1), (1, -2), (1, 2), (0, -3), (0, 3),
+    (1, -3), (1, 3), (0, 4), (1, 4),
 )
 BACK = (
-    (1, 0), (0, -1), (0, 1), (1, -1),
-    (1, 4), (0, 4), (1, 3), (1, -3), (0, 3), (0, -3), (1, 2), (1, -2), (1, 1), (0, 2), (0, -2),
+    (1, -1), (1, -2), (1, 4), (0, 4), (1, -3), (1, 3), (1, 1), (0, 3), (0, -3), (1, 2),
+    (0, 2), (0, 1), (0, -2), (0, -1), (1, 0),
 )
-SENDS = tuple([(3, (1, -1))] + [(n, BACK[n]) for n in range(4, 15)] + [(14, x) for x in BACK[:3]])
-BOTH, ROW0, ROW1 = (0, 1), (0,), (1,)
+SENDS = {
+    (1, -1): (0, 0), (1, 4): (2, 2), (0, 4): (3, 3), (1, -3): (4, 4), (1, 3): (5, 5), (1, 1): (6, 6), (0, 3): (7, 7),
+    (0, -3): (8, 8), (1, -2): (8, 8), (1, 2): (10, 10), (0, 2): (13, 11), (0, 1): (11, 11), (0, -2): (13, 13),
+    (0, -1): (13, 13), (1, 0): (14, 14),
+}
 ARRIVALS = (
-    ((ROW0, (0, -2)), (ROW0, (0, 2)), (BOTH, (0, -1)), (BOTH, (0, 1)), (ROW1, (1, 0))),
-    ((ROW1, (1, -2)), (ROW1, (1, 2)), (BOTH, (0, -3), 0), (BOTH, (0, 3), 0), (ROW1, (0, -2)), (ROW1, (0, 2)),
-     (ROW1, (1, -1)), (ROW1, (1, 1))),
-    ((ROW1, (1, -3)), (ROW1, (1, 3)), (ROW1, (0, -3)), (ROW1, (0, 3)), (ROW0, (0, 4))),
-    ((ROW1, (0, 4)), (ROW1, (1, 4))),
+    ((0, -2), (0, 2), (0, -1), (0, 1), (1, 0)),
+    ((1, -2), (1, 2), (0, -3), (0, 3), (1, -1), (1, 1)),
+    ((1, -3), (1, 3), (0, 4), (1, 4)),
 )
-KEY_STEPS = (0, 3, 9, 13)
-VALUE_STEPS = (5, 10, 14, None)
-LAST_VALUES = 2
+KEY_STEPS = (0, 3, 9)
+VALUE_STEPS = (3, 9)
 
 
 def slot_id(r, d):
@@ -49,13 +48,11 @@
 SLOTS = tuple(slot_id(r, d) for r, d in ORDER)
 
 RAW_EDGES = (
+    ((0, -2), (0, 0), 2, 0, lambda r, z: True),
+    ((0, 2), (0, 0), -2, 0, lambda r, z: True),
     ((0, -1), (0, 0), 1, 0, lambda r, z: True),
-    ((0, -2), (0, 0), 2, 0, lambda r, z: r == 0),
     ((0, 1), (0, 0), -1, 0, lambda r, z: True),
-    ((0, 2), (0, 0), -2, 0, lambda r, z: r == 0),
     ((1, 0), (0, 0), 0, 1, lambda r, z: r == 1),
-    ((0, -2), (0, -1), 1, 0, lambda r, z: r == 1),
-    ((0, 2), (0, 1), -1, 0, lambda r, z: r == 1),
     ((1, -2), (0, -2), 0, 1, lambda r, z: r == 1),
     ((1, 2), (0, 2), 0, 1, lambda r, z: r == 1),
     ((1, -1), (0, -1), 0, 1, lambda r, z: r == 1),
@@ -66,10 +63,10 @@
     ((1, -3), (1, -2), 1, 0, lambda r, z: r == 1 and z < 3),
     ((1, 3), (1, 2), -1, 0, lambda r, z: r == 1),
     ((0, 4), (0, -3), 1, 0, lambda r, z: True),
-    ((1, 4), (1, -3), 1, 0, lambda r, z: r == 1 and 4 <= z < 7),
-    ((1, 4), (0, 4), 0, 1, lambda r, z: r == 1 and z == 7),
-    ((1, 4), (1, 3), -1, 0, lambda r, z: r == 1 and z < 4),
+    ((1, 4), (1, -2), 2, 0, lambda r, z: r == 1 and z >= 4),
+    ((1, 4), (1, 2), -2, 0, lambda r, z: r == 1 and z < 4),
 )
+HALF_EDGE = 15
 
 
 def plan():
@@ -105,6 +102,8 @@
     for r, d in ORDER
 )
 EDGES = tuple((slot_id(*t), slot_id(*p), dz, dy) for t, p, dz, dy, _ in RAW_EDGES)
+for child, parent, _, _, _ in RAW_EDGES:
+    assert parent == (0, 0) or all(a < b for a in SENDS[child] for b in SENDS[parent])
 NEED_MASKS = dict(zip(SLOTS, NEEDED))
 SLOT_MASKS = {s: sum(m for m, e in zip(MASKS, EDGES) if e[0] == s) for s in range(16)}
 
@@ -149,6 +148,12 @@
         load.start()
     kall[OWN] = k[...]
     vall[OWN] = v[...]
+
+    @pl.when(in_mask(MASKS[HALF_EDGE], me))
+    def _():
+        kall[EDGES[HALF_EDGE][0], : ROWS // 2] = jnp.zeros((ROWS // 2, HEAD), jnp.bfloat16)
+        vall[EDGES[HALF_EDGE][0], : ROWS // 2] = jnp.zeros((ROWS // 2, HEAD), jnp.bfloat16)
+
     pl.semaphore_wait(barrier, len(near))
 
     def remote(src, dst, ssem, rsem, target):
@@ -157,6 +162,9 @@
             device_id={"ctx": target}, device_id_type=pl.DeviceIdType.MESH,
         )
 
+    def rows_of(n):
+        return pl.ds(ROWS // 2, ROWS // 2) if n == HALF_EDGE else pl.ds(0, ROWS)
+
     gathers = ((kall, kgs, kgr), (vall, vgs, vgr))
 
     def forward(which, s):
@@ -167,21 +175,29 @@
 
                 @pl.when(in_mask(MASKS[n], target))
                 def _(n=n, t=t, target=target):
-                    remote(buf.at[s], buf.at[t], ssem.at[n], rsem.at[t], target).start()
+                    part = rows_of(n)
+                    remote(buf.at[s, part], buf.at[t, part], ssem.at[n], rsem.at[t], target).start()
 
     def arrive(which, stage):
         buf, _, rsem = gathers[which]
-        for rows, (r, d), *only in ARRIVALS[stage]:
+        for r, d in ARRIVALS[stage]:
             s = slot_id(r, d)
-            mask = SLOT_MASKS[s] & sum(0xFF << (RING * n) for n in (only or rows))
-            if mask:
-
-                @pl.when(in_mask(mask, me))
+            for n, edge in enumerate(EDGES):
+                if edge[0] == s and MASKS[n]:
+
+                    @pl.when(in_mask(MASKS[n], me))
+                    def _(n=n):
+                        part = rows_of(n)
+                        remote(buf.at[s, part], buf.at[s, part], here.at[0], rsem.at[s], me).wait_recv()
+
+            if SLOT_MASKS[s]:
+
+                @pl.when(in_mask(SLOT_MASKS[s], me))
                 def _(s=s):
-                    remote(buf.at[s], buf.at[s], here.at[0], rsem.at[s], me).wait_recv()
                     forward(which, s)
 
     forward(0, OWN)
+    forward(1, OWN)
     for load in loads:
         load.wait()
 
@@ -248,15 +264,14 @@
 
     @pl.loop(0, 15)
     def _(step):
-        for stage in range(4):
-            for which, steps in ((0, KEY_STEPS), (1, VALUE_STEPS)):
-                if steps[stage] is not None:
-
-                    @pl.when(step == steps[stage])
-                    def _(which=which, stage=stage):
+        for n in range(15):
+            due = [(w, i) for w, steps in ((0, KEY_STEPS), (1, VALUE_STEPS)) for i, at in enumerate(steps) if at == n]
+            if due:
+
+                @pl.when(step == n)
+                def _(due=due):
+                    for which, stage in due:
                         arrive(which, stage)
-                        if which == 0 and stage == 0:
-                            forward(1, OWN)
 
         @pl.when(in_mask(pick(step, NEEDED), me))
         def _():
@@ -301,8 +316,9 @@
 
                     @pl.when(in_mask(MASKS[n], place(dz, dy)))
                     def _(n=n):
-                        remote(land.at[n], land.at[n], ssem.at[n], rsem.at[n], me).wait_recv()
-                        acc[s] += land[n].astype(jnp.float32)
+                        part = rows_of(n)
+                        remote(land.at[n, part], land.at[n, part], ssem.at[n], rsem.at[n], me).wait_recv()
+                        acc[s, part] += land[n, part].astype(jnp.float32)
 
             if s == OWN:
                 continue
@@ -312,7 +328,8 @@
 
                     @pl.when(in_mask(MASKS[n], me))
                     def _(n=n, dz=dz, dy=dy):
-                        remote(out.at[s], land.at[n], ssem.at[n], rsem.at[n], place(-dz, dy)).start()
+                        part = rows_of(n)
+                        remote(out.at[s, part], land.at[n, part], ssem.at[n], rsem.at[n], place(-dz, dy)).start()
 
     for s in SLOTS:
         relay = SLOT_MASKS[s] & ~NEED_MASKS[s]
@@ -323,26 +340,37 @@
                 acck[s] = jnp.zeros((ROWS, HEAD), jnp.float32)
                 accv[s] = jnp.zeros((ROWS, HEAD), jnp.float32)
 
+    @pl.when(row == 0)
+    def _():
+        arrive(1, 2)
+
     stage_a(following(jnp.int32(-1)), 0)
 
     def returning(step, half):
         use = in_mask(pick(step, tuple(NEED_MASKS[s] for s in back)), me)
 
-        @pl.when(step == LAST_VALUES)
+        @pl.when((step == 1) & (row == 1))
         def _():
-            arrive(1, 3)
+            arrive(1, 2)
 
         @pl.when(use)
         def _():
             stage_a(following(step), 1 - half)
             stage_b(pick(step, back), half)
 
-        for n, slot in SENDS:
-            s = slot_id(*slot)
-
-            @pl.when((step == n) & in_mask(SLOT_MASKS[s], me))
-            def _(s=s):
-                add_children(s)
+        for n in range(15):
+            due = [(slot_id(*slot), r) for slot, at in SENDS.items() for r in (0, 1) if at[r] == n]
+            due = [(s, SLOT_MASKS[s] & (0xFF << (RING * r))) for s, r in due]
+            if due:
+
+                @pl.when(step == n)
+                def _(due=due):
+                    for s, mask in due:
+                        if mask:
+
+                            @pl.when(in_mask(mask, me))
+                            def _(s=s):
+                                add_children(s)
 
         return jnp.where(use, 1 - half, half)
 
@@ -362,13 +390,15 @@
 
             @pl.when(in_mask(MASKS[n], place(dz, dy)))
             def _(n=n):
+                part = rows_of(n)
                 for buf, ssem, rsem in gathers:
-                    remote(buf.at[0], buf.at[0], ssem.at[n], rsem.at[0], me).wait_send()
+                    remote(buf.at[0, part], buf.at[0, part], ssem.at[n], rsem.at[0], me).wait_send()
 
             @pl.when(in_mask(MASKS[n], me))
             def _(n=n):
+                part = rows_of(n)
                 for _, out, land, ssem, rsem in returns:
-                    remote(out.at[0], land.at[n], ssem.at[n], rsem.at[n], me).wait_send()
+                    remote(out.at[0, part], land.at[n, part], ssem.at[n], rsem.at[n], me).wait_send()
 
     store.wait()
 

time: 62.1 us -> 59.4 us (0.957); the launches traced: 61.8 us -> 58.3 us
  Pallas kernels: 61.2 us -> 57.6 us
    pallas_call x1, Pallas kernels: 59.3 us -> 55.7 us  [local(): pl.pallas_call(kernel, out_shape=shapes, in_specs=[pl.BlockSpec(memory_sp...]
where the time goes in v3:
time: 59.4 us; the launch traced here: 58.3 us
  Pallas kernels  57.6 us (97%)
  between operations  0.64 us (1%)
    pallas_call x1, Pallas kernels, local(): pl.pallas_call(kernel, out_shape=shapes, in_specs=[pl.BlockSpec(memory_sp...  55.7 us
    pallas_call x1, Pallas kernels, local(): pl.pallas_call(hand_over, out_shape=shapes, in_specs=[vmem] * 3, out_spec...  1.92 us

profile of v3, /device:TPU:36, one launch (start us, length us, event | category | flops | bytes accessed | tf_op | source)
XLA Modules:
  0.0 58.3 jit_solution(7344150323443008446)
XLA Ops:
  0.6 55.7 %attention_backward.1 = (bf16[256,1024]{1,0:T(8,128)(2,1)}, bf16[256,128]{1,0:T(8,128)(2,1)}, bf16[256,128]{1,0:T(8,128)(2,1)}) custom-call(s32[32]{0:T(128)} %docs.1, bf16[256,1024]{1,0:T(8,128)(2,1)} %q_any.1, bf16[256,128]{1,0:T(8,128)(2,1)} %k.1, bf16[256,128]{1,0:T(8,128)(2,1)} %v.1, bf16[256,1024]{1,0:T(8,128)(2,1)} %o_any.1, bf16[256,1024]{1,0:T(8,128)(2,1)} %do_any.1), custom_call_target="tpu_custom_call" | custom-call | tf_op jit(solution)/shard_map/attention_backward/pallas_call | solution.py:421
  56.3 1.9 %hand_over.1 = (bf16[256,1024]{1,0:T(8,128)(2,1)}, bf16[256,128]{1,0:T(8,128)(2,1)}, bf16[256,128]{1,0:T(8,128)(2,1)}) custom-call(bf16[256,1024]{1,0:T(8,128)(2,1)} %get-tuple-element.6.dq, bf16[256,128]{1,0:T(8,128)(2,1)} %get-tuple-element.7.dk, bf16[256,128]{1,0:T(8,128)(2,1)} %get-tuple-element.8.dv), custom_call_target="tpu_custom_call" | custom-call | tf_op jit(solution)/shard_map/hand_over/pallas_call | solution.py:456

commit v4 on v3

--- a/solution.py
+++ b/solution.py
@@ -24,13 +24,13 @@
     (1, -3), (1, 3), (0, 4), (1, 4),
 )
 BACK = (
-    (1, -1), (1, -2), (1, 4), (0, 4), (1, -3), (1, 3), (1, 1), (0, 3), (0, -3), (1, 2),
-    (0, 2), (0, 1), (0, -2), (0, -1), (1, 0),
+    (1, -1), (1, -2), (1, 4), (0, 4), (1, -3), (0, -1), (1, 3), (0, -3), (0, 3), (1, 1),
+    (1, 2), (0, 2), (0, -2), (0, 1), (1, 0),
 )
 SENDS = {
-    (1, -1): (0, 0), (1, 4): (2, 2), (0, 4): (3, 3), (1, -3): (4, 4), (1, 3): (5, 5), (1, 1): (6, 6), (0, 3): (7, 7),
-    (0, -3): (8, 8), (1, -2): (8, 8), (1, 2): (10, 10), (0, 2): (13, 11), (0, 1): (11, 11), (0, -2): (13, 13),
-    (0, -1): (13, 13), (1, 0): (14, 14),
+    (1, -1): (0, 0), (1, 4): (2, 2), (0, 4): (3, 3), (1, -3): (4, 4), (0, -1): (5, 5), (1, 3): (6, 6), (0, -3): (8, 8),
+    (1, -2): (8, 8), (0, 3): (8, 8), (1, 1): (9, 9), (1, 2): (10, 10), (0, 2): (14, 12), (0, -2): (13, 12),
+    (0, 1): (13, 13), (1, 0): (14, 14),
 }
 ARRIVALS = (
     ((0, -2), (0, 2), (0, -1), (0, 1), (1, 0)),
@@ -38,7 +38,7 @@
     ((1, -3), (1, 3), (0, 4), (1, 4)),
 )
 KEY_STEPS = (0, 3, 9)
-VALUE_STEPS = (3, 9)
+VALUE_STEPS = (5,10)
 
 
 def slot_id(r, d):
@@ -104,6 +104,10 @@
 EDGES = tuple((slot_id(*t), slot_id(*p), dz, dy) for t, p, dz, dy, _ in RAW_EDGES)
 for child, parent, _, _, _ in RAW_EDGES:
     assert parent == (0, 0) or all(a < b for a in SENDS[child] for b in SENDS[parent])
+TILE = ROWS // 2
+FAR = slot_id(1, 4)
+FAR_MASK = MASKS[HALF_EDGE]
+NEEDED = tuple(m & ~FAR_MASK if s == FAR else m for s, m in zip(SLOTS, NEEDED))
 NEED_MASKS = dict(zip(SLOTS, NEEDED))
 SLOT_MASKS = {s: sum(m for m, e in zip(MASKS, EDGES) if e[0] == s) for s in range(16)}
 
@@ -122,7 +126,7 @@
 def kernel(
     docs, q_any, k, v, o_any, do_any, dq_any, dk, dv,
     q, o, do, dq, qt, dot_, qb, dob, kall, vall, ebuf, seen, top, total, lse, dqt, pbuf, dsbuf, acck, accv,
-    sendk, sendv, landk, landv, kgs, kgr, vgs, vgr, krs, krr, vrs, vrr, here,
+    sendk, sendv, landk, landv, pfar, dsfar, kgs, kgr, vgs, vgr, krs, krr, vrs, vrr, here,
 ):
     me = lax.axis_index("ctx")
     row = me // RING
@@ -148,12 +152,6 @@
         load.start()
     kall[OWN] = k[...]
     vall[OWN] = v[...]
-
-    @pl.when(in_mask(MASKS[HALF_EDGE], me))
-    def _():
-        kall[EDGES[HALF_EDGE][0], : ROWS // 2] = jnp.zeros((ROWS // 2, HEAD), jnp.bfloat16)
-        vall[EDGES[HALF_EDGE][0], : ROWS // 2] = jnp.zeros((ROWS // 2, HEAD), jnp.bfloat16)
-
     pl.semaphore_wait(barrier, len(near))
 
     def remote(src, dst, ssem, rsem, target):
@@ -197,7 +195,6 @@
                     forward(which, s)
 
     forward(0, OWN)
-    forward(1, OWN)
     for load in loads:
         load.wait()
 
@@ -260,6 +257,25 @@
             seen[s, :, sl] = new
             ebuf[s, h] = e.reshape(ROWS, ROWS)
 
+    def pairs():
+        for h in range(0, HEADS, 2):
+            yield h, slice(h * ROWS, h * ROWS + TILE), slice((h + 1) * ROWS, (h + 1) * ROWS + TILE)
+
+    def first_pass_far():
+        hot = jnp.where(lane[:TILE] == docs[2 * block_of(FAR) + 1], 1.0, 0.0).astype(jnp.bfloat16)
+        ka = jnp.concatenate([kall[FAR, TILE:], hot], axis=1)
+        for h, one, two in pairs():
+            both = dot(ka, jnp.concatenate([qt[:, one], qt[:, two]], axis=1))
+            for n, sl in enumerate((one, two)):
+                score = both[:, n * TILE : (n + 1) * TILE].reshape(TILE // 8, 8, TILE)
+                old = top[:, sl]
+                new = jnp.maximum(old, jnp.max(score, axis=0))
+                e = jnp.exp2((score - new[None]) * LOG2_SCALE)
+                total[:, sl] = jnp.sum(e, axis=0) + total[:, sl] * jnp.exp2((old - new) * LOG2_SCALE)
+                top[:, sl] = new
+                seen[FAR, :, sl] = new
+                ebuf[FAR, h + n, :TILE, :TILE] = e.reshape(TILE, TILE)
+
     first_pass(OWN, True)
 
     @pl.loop(0, 15)
@@ -272,10 +288,16 @@
                 def _(due=due):
                     for which, stage in due:
                         arrive(which, stage)
+                        if which == 0 and stage == 0:
+                            forward(1, OWN)
 
         @pl.when(in_mask(pick(step, NEEDED), me))
         def _():
             first_pass(pick(step, SLOTS), False)
+
+        @pl.when((step == SLOTS.index(FAR)) & in_mask(FAR_MASK, me))
+        def _():
+            first_pass_far()
 
     peak = jnp.max(top[...], axis=0, keepdims=True)
     norm = jnp.sum(total[...] * jnp.exp2((top[...] - peak) * LOG2_SCALE), axis=0, keepdims=True)
@@ -299,6 +321,24 @@
         acck[s] = dot(dsbuf[half], qb[...])
         dqt[...] += dot(kall[s].T, dsbuf[half])
 
+    def second_pass_far():
+        va = jnp.concatenate([vall[FAR, TILE:], ones[:TILE]], axis=1)
+        for h, one, two in pairs():
+            both = dot(va, jnp.concatenate([dot_[:, one], dot_[:, two]], axis=1))
+            for n, sl in enumerate((one, two)):
+                factor = jnp.exp2((seen[FAR, :, sl] - top[:, sl]) * LOG2_SCALE - lse[:, sl])
+                prob = ebuf[FAR, h + n, :TILE, :TILE].reshape(TILE // 8, 8, TILE) * factor[None]
+                prob = prob.reshape(TILE, TILE)
+                cols = slice((h + n) * TILE, (h + n + 1) * TILE)
+                pfar[:, cols] = prob.astype(jnp.bfloat16)
+                dsfar[:, cols] = (prob * both[:, n * TILE : (n + 1) * TILE]).astype(jnp.bfloat16)
+        firsts = [slice(h * ROWS, h * ROWS + TILE) for h in range(HEADS)]
+        accv[FAR, TILE:] = dot(pfar[...], jnp.concatenate([dob[sl, :] for sl in firsts], axis=0))
+        acck[FAR, TILE:] = dot(dsfar[...], jnp.concatenate([qb[sl, :] for sl in firsts], axis=0))
+        part = dot(kall[FAR, TILE:].T, dsfar[...])
+        for h, sl in enumerate(firsts):
+            dqt[:, sl] += part[:, h * TILE : (h + 1) * TILE]
+
     back = tuple(slot_id(r, d) for r, d in BACK)
 
     def following(step):
@@ -357,6 +397,10 @@
         def _():
             stage_a(following(step), 1 - half)
             stage_b(pick(step, back), half)
+
+        @pl.when((step == back.index(FAR)) & in_mask(FAR_MASK, me))
+        def _():
+            second_pass_far()
 
         for n in range(15):
             due = [(slot_id(*slot), r) for slot, at in SENDS.items() for r in (0, 1) if at[r] == n]
@@ -445,6 +489,8 @@
             pltpu.VMEM((16, ROWS, HEAD), bf16),
             pltpu.VMEM((len(EDGES), ROWS, HEAD), bf16),
             pltpu.VMEM((len(EDGES), ROWS, HEAD), bf16),
+            pltpu.VMEM((TILE, HEADS * TILE), bf16),
+            pltpu.VMEM((TILE, HEADS * TILE), bf16),
         ]
         + [pltpu.SemaphoreType.DMA((len(EDGES),))] * 8
         + [pltpu.SemaphoreType.DMA((3,))],

time: 59.4 us -> 57 us (0.960); the launches traced: 58.3 us -> 56.8 us
  Pallas kernels: 57.6 us -> 56.2 us
    pallas_call x1, Pallas kernels: 55.7 us -> 54.2 us  [local(): pl.pallas_call(kernel, out_shape=shapes, in_specs=[pl.BlockSpec(memory_sp...]
where the time goes in v4:
time: 57 us; the launch traced here: 56.8 us
  Pallas kernels  56.2 us (99%)
  between operations  0.64 us (1%)
    pallas_call x1, Pallas kernels, local(): pl.pallas_call(kernel, out_shape=shapes, in_specs=[pl.BlockSpec(memory_sp...  54.2 us
    pallas_call x1, Pallas kernels, local(): pl.pallas_call(hand_over, out_shape=shapes, in_specs=[vmem] * 3, out_spec...  1.92 us

profile of v4, /device:TPU:36, one launch (start us, length us, event | category | flops | bytes accessed | tf_op | source)
XLA Modules:
  0.0 56.8 jit_solution(4331514341037964972)
XLA Ops:
  0.6 54.2 %attention_backward.1 = (bf16[256,1024]{1,0:T(8,128)(2,1)}, bf16[256,128]{1,0:T(8,128)(2,1)}, bf16[256,128]{1,0:T(8,128)(2,1)}) custom-call(s32[32]{0:T(128)} %docs.1, bf16[256,1024]{1,0:T(8,128)(2,1)} %q_any.1, bf16[256,128]{1,0:T(8,128)(2,1)} %k.1, bf16[256,128]{1,0:T(8,128)(2,1)} %v.1, bf16[256,1024]{1,0:T(8,128)(2,1)} %o_any.1, bf16[256,1024]{1,0:T(8,128)(2,1)} %do_any.1), custom_call_target="tpu_custom_call" | custom-call | tf_op jit(solution)/shard_map/attention_backward/pallas_call | solution.py:465
  54.9 1.9 %hand_over.1 = (bf16[256,1024]{1,0:T(8,128)(2,1)}, bf16[256,128]{1,0:T(8,128)(2,1)}, bf16[256,128]{1,0:T(8,128)(2,1)}) custom-call(bf16[256,1024]{1,0:T(8,128)(2,1)} %get-tuple-element.6.dq, bf16[256,128]{1,0:T(8,128)(2,1)} %get-tuple-element.7.dk, bf16[256,128]{1,0:T(8,128)(2,1)} %get-tuple-element.8.dv), custom_call_target="tpu_custom_call" | custom-call | tf_op jit(solution)/shard_map/hand_over/pallas_call | solution.py:502

commit v5 on v4

--- a/solution.py
+++ b/solution.py
@@ -124,8 +124,8 @@
 
 
 def kernel(
-    docs, q_any, k, v, o_any, do_any, dq_any, dk, dv,
-    q, o, do, dq, qt, dot_, qb, dob, kall, vall, ebuf, seen, top, total, lse, dqt, pbuf, dsbuf, acck, accv,
+    docs_any, q_any, k_any, v_any, o_any, do_any, dq_any, dk, dv,
+    docs, q, o, do, dq, qt, dot_, qb, dob, kall, vall, ebuf, seen, top, total, lse, dqt, pbuf, dsbuf, acck, accv,
     sendk, sendv, landk, landv, pfar, dsfar, kgs, kgr, vgs, vgr, krs, krr, vrs, vrr, here,
 ):
     me = lax.axis_index("ctx")
@@ -146,12 +146,15 @@
 
     loads = [
         pltpu.make_async_copy(src, dst, here.at[n])
-        for n, (src, dst) in enumerate(((q_any, q), (do_any, do), (o_any, o)))
+        for n, (src, dst) in enumerate(
+            (
+                (k_any, kall.at[OWN]), (v_any, vall.at[OWN]), (docs_any, docs),
+                (q_any, q), (do_any, do), (o_any, o),
+            )
+        )
     ]
     for load in loads:
         load.start()
-    kall[OWN] = k[...]
-    vall[OWN] = v[...]
     pl.semaphore_wait(barrier, len(near))
 
     def remote(src, dst, ssem, rsem, target):
@@ -174,7 +177,8 @@
                 @pl.when(in_mask(MASKS[n], target))
                 def _(n=n, t=t, target=target):
                     part = rows_of(n)
-                    remote(buf.at[s, part], buf.at[t, part], ssem.at[n], rsem.at[t], target).start()
+                    src = (k_any, v_any)[which] if s == OWN else buf.at[s, part]
+                    remote(src, buf.at[t, part], ssem.at[n], rsem.at[t], target).start()
 
     def arrive(which, stage):
         buf, _, rsem = gathers[which]
@@ -465,9 +469,10 @@
     results = pl.pallas_call(
         kernel,
         out_shape=shapes,
-        in_specs=[pl.BlockSpec(memory_space=pltpu.SMEM), any_, vmem, vmem, any_, any_],
+        in_specs=[any_] * 6,
         out_specs=(any_, vmem, vmem),
-        scratch_shapes=[pltpu.VMEM((ROWS, HEADS * HEAD), bf16)] * 4
+        scratch_shapes=[pltpu.SMEM((2 * RING * 2,), jnp.int32)]
+        + [pltpu.VMEM((ROWS, HEADS * HEAD), bf16)] * 4
         + [
             pltpu.VMEM((2 * HEAD, WIDE), bf16),
             pltpu.VMEM((2 * HEAD, WIDE), bf16),
@@ -493,7 +498,7 @@
             pltpu.VMEM((TILE, HEADS * TILE), bf16),
         ]
         + [pltpu.SemaphoreType.DMA((len(EDGES),))] * 8
-        + [pltpu.SemaphoreType.DMA((3,))],
+        + [pltpu.SemaphoreType.DMA((6,))],
         compiler_params=pltpu.CompilerParams(
             collective_id=0, has_side_effects=True, vmem_limit_bytes=60 * 2**20
         ),

time: 57 us -> 55.6 us (0.975)
  Pallas kernels: 56.2 us -> 54.8 us
    pallas_call x1, Pallas kernels: 54.2 us -> 52.8 us  [local(): pl.pallas_call(kernel, out_shape=shapes, in_specs=[any_] * 6, out_specs=(...]
where the time goes in v5:
time: 55.6 us; the launch traced here: 55.4 us
  Pallas kernels  54.8 us (99%)
  between operations  0.64 us (1%)
    pallas_call x1, Pallas kernels, local(): pl.pallas_call(kernel, out_shape=shapes, in_specs=[any_] * 6, out_specs=(...  52.8 us
    pallas_call x1, Pallas kernels, local(): pl.pallas_call(hand_over, out_shape=shapes, in_specs=[vmem] * 3, out_spec...  1.92 us

profile of v5, /device:TPU:36, one launch (start us, length us, event | category | flops | bytes accessed | tf_op | source)
XLA Modules:
  0.0 55.4 jit_solution(9435760093801259357)
XLA Ops:
  0.6 52.8 %attention_backward.1 = (bf16[256,1024]{1,0:T(8,128)(2,1)}, bf16[256,128]{1,0:T(8,128)(2,1)}, bf16[256,128]{1,0:T(8,128)(2,1)}) custom-call(s32[32]{0:T(128)} %docs_any.1, bf16[256,1024]{1,0:T(8,128)(2,1)} %q_any.1, bf16[256,128]{1,0:T(8,128)(2,1)} %k_any.1, bf16[256,128]{1,0:T(8,128)(2,1)} %v_any.1, bf16[256,1024]{1,0:T(8,128)(2,1)} %o_any.1, ...), custom_call_target="tpu_custom_call" | custom-call | tf_op jit(solution)/shard_map/attention_backward/pallas_call | solution.py:469
  53.5 1.9 %hand_over.1 = (bf16[256,1024]{1,0:T(8,128)(2,1)}, bf16[256,128]{1,0:T(8,128)(2,1)}, bf16[256,128]{1,0:T(8,128)(2,1)}) custom-call(bf16[256,1024]{1,0:T(8,128)(2,1)} %get-tuple-element.6.dq, bf16[256,128]{1,0:T(8,128)(2,1)} %get-tuple-element.7.dk, bf16[256,128]{1,0:T(8,128)(2,1)} %get-tuple-element.8.dv), custom_call_target="tpu_custom_call" | custom-call | tf_op jit(solution)/shard_map/hand_over/pallas_call | solution.py:507

commit v6 on v5

--- a/solution.py
+++ b/solution.py
@@ -124,7 +124,7 @@
 
 
 def kernel(
-    docs_any, q_any, k_any, v_any, o_any, do_any, dq_any, dk, dv,
+    docs_any, q_any, k_any, v_any, o_any, do_any, dq_any, dk_any, dv_any,
     docs, q, o, do, dq, qt, dot_, qb, dob, kall, vall, ebuf, seen, top, total, lse, dqt, pbuf, dsbuf, acck, accv,
     sendk, sendv, landk, landv, pfar, dsfar, kgs, kgr, vgs, vgr, krs, krr, vrs, vrr, here,
 ):
@@ -430,8 +430,15 @@
     store = pltpu.make_async_copy(dq, dq_any, here.at[0])
     store.start()
     add_children(OWN)
-    dv[...] = accv[OWN].astype(jnp.bfloat16)
-    dk[...] = (acck[OWN] * SCALE).astype(jnp.bfloat16)
+    sendv[OWN] = accv[OWN].astype(jnp.bfloat16)
+    sendk[OWN] = (acck[OWN] * SCALE).astype(jnp.bfloat16)
+    stores = [
+        store,
+        pltpu.make_async_copy(sendv.at[OWN], dv_any, here.at[1]),
+        pltpu.make_async_copy(sendk.at[OWN], dk_any, here.at[2]),
+    ]
+    for copy in stores[1:]:
+        copy.start()
 
     for n, (t, parent, dz, dy) in enumerate(EDGES):
         if MASKS[n]:
@@ -448,7 +455,8 @@
                 for _, out, land, ssem, rsem in returns:
                     remote(out.at[0, part], land.at[n, part], ssem.at[n], rsem.at[n], me).wait_send()
 
-    store.wait()
+    for copy in stores:
+        copy.wait()
 
 
 def hand_over(dq, dk, dv, dq_out, dk_out, dv_out):
@@ -470,7 +478,7 @@
         kernel,
         out_shape=shapes,
         in_specs=[any_] * 6,
-        out_specs=(any_, vmem, vmem),
+        out_specs=(any_,) * 3,
         scratch_shapes=[pltpu.SMEM((2 * RING * 2,), jnp.int32)]
         + [pltpu.VMEM((ROWS, HEADS * HEAD), bf16)] * 4
         + [

time: 55.6 us -> 55.4 us (level)
  no operation moved by 1% of the time
where the time goes in v6:
time: 55.4 us; the launch traced here: 55.2 us
  Pallas kernels  54.6 us (99%)
  between operations  0.64 us (1%)
    pallas_call x1, Pallas kernels, local(): pl.pallas_call(kernel, out_shape=shapes, in_specs=[any_] * 6, out_specs=(...  52.7 us
    pallas_call x1, Pallas kernels, local(): pl.pallas_call(hand_over, out_shape=shapes, in_specs=[vmem] * 3, out_spec...  1.92 us

profile of v6, /device:TPU:36, one launch (start us, length us, event | category | flops | bytes accessed | tf_op | source)
XLA Modules:
  0.0 55.2 jit_solution(13771729414276513772)
XLA Ops:
  0.6 52.7 %attention_backward.1 = (bf16[256,1024]{1,0:T(8,128)(2,1)}, bf16[256,128]{1,0:T(8,128)(2,1)}, bf16[256,128]{1,0:T(8,128)(2,1)}) custom-call(s32[32]{0:T(128)} %docs_any.1, bf16[256,1024]{1,0:T(8,128)(2,1)} %q_any.1, bf16[256,128]{1,0:T(8,128)(2,1)} %k_any.1, bf16[256,128]{1,0:T(8,128)(2,1)} %v_any.1, bf16[256,1024]{1,0:T(8,128)(2,1)} %o_any.1, ...), custom_call_target="tpu_custom_call" | custom-call | tf_op jit(solution)/shard_map/attention_backward/pallas_call | solution.py:477
  53.3 1.9 %hand_over.1 = (bf16[256,1024]{1,0:T(8,128)(2,1)}, bf16[256,128]{1,0:T(8,128)(2,1)}, bf16[256,128]{1,0:T(8,128)(2,1)}) custom-call(bf16[256,1024]{1,0:T(8,128)(2,1)} %get-tuple-element.6.dq, bf16[256,128]{1,0:T(8,128)(2,1)} %get-tuple-element.7.dk, bf16[256,128]{1,0:T(8,128)(2,1)} %get-tuple-element.8.dv), custom_call_target="tpu_custom_call" | custom-call | tf_op jit(solution)/shard_map/hand_over/pallas_call | solution.py:515
